TPU v7x, 32 devices: a whole 2x2x4 slice. The times are simulated.
32 devices in a mesh: dp: 4 (over z), table: 8 (over y, x, core).
Axes of the slice: x: 2, y: 2, z: 4, core: 2. Of those that a mesh axis runs over, the one named last changes fastest.
Arguments:
- core_ids: int32 [4096, 8, 3, 2], P(('dp', 'table')), may hold values from 0 to 249
- bag_lengths: int32 [4096, 8], P(('dp', 'table')), may hold values from 1 to 2
- first_core: bfloat16 [8, 250, 512], P('table'), may hold values from -6 to 6
- middle_core: bfloat16 [8, 250, 64, 128], P('table'), may hold values from -0.75 to 0.75
- last_core: bfloat16 [8, 250, 512], P('table'), may hold values from -0.75 to 0.75
- grad_hidden: bfloat16 [4096, 1024], P(('dp', 'table')), may hold values from -0.1875 to 0.1875
Outputs:
- pooled: bfloat16 [4096, 1024], P(('dp', 'table'))
- weight_grad: float32 [1024, 1024], P('table', 'dp')
Inputs may be any that keep to these rules, and one draw needn't show every extreme that they name: `core_ids`: slots j >= bag_lengths[n, t] hold ids that are not used.
All inputs are finite; a program needn't handle non-finite values.
Results may differ from a plain program's by a relative error of at most 0.005.
Values may be sent and summed in bfloat16 or wider, within the bound.
A program may use at most 128 MiB of HBM per device.

v0:
```python
import jax
import jax.numpy as jnp
from jax import lax
from jax.sharding import PartitionSpec as P

D1 = 8
D2 = 2
D3 = 8
RANK = 64
BAG = 2


def build_rows(wanted, counts, first, middle, last):
    block = wanted.shape[0]
    head = jnp.take(first, wanted[:, 0, :], axis=0).reshape(block, BAG, D1, RANK)
    centre = jnp.take(middle, wanted[:, 1, :], axis=0)
    prefix = jnp.einsum("njar,njrs->njas", head, centre, preferred_element_type=jnp.float32)
    prefix = prefix.astype(jnp.bfloat16).reshape(block, BAG, D1 * D2, RANK)
    tail = jnp.take(last, wanted[:, 2, :], axis=0).reshape(block, BAG, RANK, D3)
    rows = jnp.einsum("njps,njsc->njpc", prefix, tail, preferred_element_type=jnp.float32)
    rows = rows.reshape(block, BAG, D1 * D2 * D3)
    live = (jnp.arange(BAG, dtype=jnp.int32)[None, :] < counts[:, None]).astype(jnp.float32)
    return jnp.sum(rows * live[:, :, None], axis=1).astype(jnp.bfloat16)


def body(core_ids, bag_lengths, first_core, middle_core, last_core, grad_hidden):
    width = D1 * D2 * D3
    got_ids, got_counts = (
        lax.all_to_all(core_ids, "table", split_axis=1, concat_axis=0, tiled=True),
        lax.all_to_all(bag_lengths, "table", split_axis=1, concat_axis=0, tiled=True),
    )
    group_rows = got_ids.shape[0]
    block = min(group_rows, 512)
    steps_count = group_rows // block
    wanted = got_ids.reshape(steps_count, block, 3, BAG)
    counts = got_counts.reshape(steps_count, block)
    first = first_core[0]
    middle = middle_core[0]
    last = last_core[0]
    table_rows = lax.map(
        lambda pair: build_rows(pair[0], pair[1], first, middle, last), (wanted, counts)
    )
    table_rows = table_rows.reshape(group_rows, width)
    returned = lax.all_to_all(
        table_rows.reshape(group_rows, 1, width), "table", split_axis=0, concat_axis=1, tiled=True
    )
    pooled = returned.reshape(returned.shape[0], returned.shape[1] * width)
    hidden_units = grad_hidden.shape[1]
    n_data = lax.axis_size("dp")
    n_tables = lax.axis_size("table")
    whole = lax.dot_general(
        pooled, grad_hidden, (((0,), (0,)), ((), ())), preferred_element_type=jnp.float32
    )
    arranged = whole.reshape(n_tables, width, n_data, hidden_units // n_data)
    arranged = jnp.transpose(arranged, (2, 0, 1, 3)).reshape(
        n_data * n_tables * width, hidden_units // n_data
    )
    weight_grad = lax.psum_scatter(arranged, ("dp", "table"), scatter_dimension=0, tiled=True)
    return (pooled, weight_grad)


def solution(mesh):
    placed = (
        P(("dp", "table"), None, None, None),
        P(("dp", "table"), None),
        P("table", None, None),
        P("table", None, None, None),
        P("table", None, None),
        P(("dp", "table"), None),
    )
    return jax.shard_map(
        body,
        mesh=mesh,
        in_specs=placed,
        out_specs=(P(("dp", "table"), None), P("table", "dp")),
        check_vma=False,
    )
```

profile of v0, /device:TPU:0, one launch (start us, length us, event | category | flops | bytes accessed | tf_op | source)
XLA Modules:
  0.0 312.5 jit_solution(11815265296601557580)
XLA Ops:
  7.2 5.2 %all-to-all-start.1 = ((s32[128,8,1]{0,2,1:T(1,128)}), s32[128,8,1]{0,2,1:T(1,128)S(1)}, u32[]{:S(2)}, u32[]{:S(2)}) async-start(s32[128,8,1]{0,2,1:T(1,128)} %bitcast.113), calls=%async_computation.1 | async-start | bytes 8192 | tf_op jit(solution)/shard_map/all_to_all | solution.py:30
  12.3 4.6 %all-to-all-done.1 = s32[128,8,1]{0,2,1:T(1,128)S(1)} async-done(((s32[128,8,1]{0,2,1:T(1,128)}), s32[128,8,1]{0,2,1:T(1,128)S(1)}, u32[]{:S(2)}, u32[]{:S(2)}) %all-to-all-start.1) | async-done | bytes 4128 | tf_op jit(solution)/shard_map/all_to_all | solution.py:30
  16.9 3.3 %all-to-all-start = ((s32[128,8,3,2]{0,3,2,1:T(2,128)}), s32[128,8,3,2]{0,3,2,1:T(2,128)S(1)}, u32[]{:S(2)}, u32[]{:S(2)}) async-start(s32[128,8,3,2]{0,3,2,1:T(2,128)} %param.10), calls=%async_computation | async-start | bytes 49152 | tf_op jit(solution)/shard_map/all_to_all | solution.py:29
  20.3 4.7 %all-to-all-done = s32[128,8,3,2]{0,3,2,1:T(2,128)S(1)} async-done(((s32[128,8,3,2]{0,3,2,1:T(2,128)}), s32[128,8,3,2]{0,3,2,1:T(2,128)S(1)}, u32[]{:S(2)}, u32[]{:S(2)}) %all-to-all-start) | async-done | bytes 24608 | tf_op jit(solution)/shard_map/all_to_all | solution.py:29
  25.0 123.5 %while.10 = (s32[]{:T(128)}, bf16[2,512,128]{2,1,0:T(8,128)(2,1)}, s32[2,512,3,2]{1,0,3,2:T(2,128)S(1)}, bf16[250,512]{1,0:T(8,128)(2,1)}, bf16[250,64,128]{2,1,...) while((s32[]{:T(128)}, bf16[2,512,128]{2,1,0:T(8,128)(2,1)}, ...), condition=%wide.region_2.4_spmd, body=%wide.region_0.3_spmd.sunk | while | flops 161710080 | bytes 95412448 | solution.py:40
  25.1 0.3 copy.107
  25.4 0.2 reshape.182
  25.6 0.4 copy-done
  26.0 4.0 %gather_fusion = bf16[1024,512]{1,0:T(8,128)(2,1)S(1)} fusion(bf16[250,512]{1,0:T(8,128)(2,1)S(1)} %copy-done, s32[1024]{0:T(1024)S(1)} %broadcast_clamp_fusion.6), kind=kCustom, calls=%fused_computation.clone.clone.1 | custom fusion | bytes 2101248 | tf_op jit(solution)/shard_map/while/body/eval_jaxpr/jit(_take)/gather | solution.py:15
  30.0 0.4 reshape.183
  30.4 1.5 copy.108
  31.9 0.2 compare_and_fusion.4
  32.1 0.1 copy.109
  32.4 2.9 copy.110
  35.3 0.2 reshape.184
  35.5 15.8 %gather_fusion.1 = bf16[1024,64,128]{2,1,0:T(8,128)(2,1)} fusion(bf16[250,64,128]{2,1,0:T(8,128)(2,1)} %get-tuple-element.176, s32[1024]{0:T(1024)S(1)} %broadcast_clamp_fusion.7), kind=kCustom, calls=%fused_computation.2.clone.1 | custom fusion | bytes 33558528 | tf_op jit(solution)/shard_map/while/body/eval_jaxpr/jit(_take)/gather | solution.py:16
  51.2 9.1 %fusion.24 = bf16[512,2,8,128]{3,2,1,0:T(8,128)(2,1)} fusion(bf16[512,2,8,64]{3,2,1,0:T(8,128)(2,1)S(1)} %copy-done.2, bf16[512,2,64,128]{3,2,1,0:T(8,128)(2,1)} %bitcast.98, pred[512,2]{1,0:T(8,128)(4,1)S(1)} %get-tuple-element.153), kind=kOutput, calls=%fused_computation.8.clone.1 | convolution fusion | flops 143654912 | bytes 19923968 | tf_op jit(solution)/shard_map/while/body/eval_jaxpr/njar,njrs->njas/dot_general | solution.py:17
  60.4 3.0 copy.111
  63.4 6.6 %copy.112 = bf16[512,2,16,64]{3,2,1,0:T(8,128)(2,1)} copy(bf16[512,2,16,64]{0,3,2,1:T(8,128)(2,1)S(1)} %bitcast.99) | data formatting | bytes 4194304 | tf_op jit(solution)/shard_map/while/body/eval_jaxpr/reshape | solution.py:18
  70.0 0.2 reshape.185
  70.2 4.0 %gather_fusion.2 = bf16[1024,512]{1,0:T(8,128)(2,1)S(1)} fusion(bf16[250,512]{1,0:T(8,128)(2,1)S(1)} %copy-done.1, s32[1024]{0:T(1024)S(1)} %broadcast_clamp_fusion.8), kind=kCustom, calls=%fused_computation.1.clone.clone.1 | custom fusion | bytes 2101248 | tf_op jit(solution)/shard_map/while/body/eval_jaxpr/jit(_take)/gather | solution.py:19
  74.2 0.4 reshape.186
  74.6 1.5 copy.113
  76.3 3.3 %copy.115 = bf16[512,2,64,8]{2,3,1,0:T(8,128)(2,1)} copy(bf16[512,2,64,8]{0,3,2,1:T(8,128)(2,1)S(1)} %select_bitcast_fusion.2) | data formatting | bytes 2097152 | tf_op jit(solution)/shard_map/while/body/eval_jaxpr/reshape | solution.py:19
  79.6 0.1 fusion.25
  79.8 5.3 %multiply_reduce_fusion.2 = bf16[512,16,8]{1,2,0:T(8,128)(2,1)S(1)} fusion(bf16[512,2,16,64]{3,2,1,0:T(8,128)(2,1)} %copy.112, bf16[512,2,64,8]{2,3,1,0:T(8,128)(2,1)} %copy.115, f32[512,2]{1,0:T(8,128)S(1)} %fusion.25), kind=kOutput, calls=%fused_computation.7.clone.1 | convolution fusion | flops 16973824 | bytes 3280896 | tf_op jit(solution)/shard_map/while/body/eval_jaxpr/njps,njsc->njpc/dot_general | solution.py:20
  85.1 0.8 copy.116
  86.1 0.7 copy-done.4
  86.8 0.3 copy.107
  87.2 0.2 reshape.182
  87.4 0.4 copy-done
  87.7 4.0 %gather_fusion = bf16[1024,512]{1,0:T(8,128)(2,1)S(1)} fusion(bf16[250,512]{1,0:T(8,128)(2,1)S(1)} %copy-done, s32[1024]{0:T(1024)S(1)} %broadcast_clamp_fusion.6), kind=kCustom, calls=%fused_computation.clone.clone.1 | custom fusion | bytes 2101248 | tf_op jit(solution)/shard_map/while/body/eval_jaxpr/jit(_take)/gather | solution.py:15
  91.7 0.4 reshape.183
  92.2 1.5 copy.108
  93.6 0.2 compare_and_fusion.4
  93.9 0.1 copy.109
  94.1 2.9 copy.110
  97.0 0.2 reshape.184
  97.2 15.8 %gather_fusion.1 = bf16[1024,64,128]{2,1,0:T(8,128)(2,1)} fusion(bf16[250,64,128]{2,1,0:T(8,128)(2,1)} %get-tuple-element.176, s32[1024]{0:T(1024)S(1)} %broadcast_clamp_fusion.7), kind=kCustom, calls=%fused_computation.2.clone.1 | custom fusion | bytes 33558528 | tf_op jit(solution)/shard_map/while/body/eval_jaxpr/jit(_take)/gather | solution.py:16
  113.0 9.1 %fusion.24 = bf16[512,2,8,128]{3,2,1,0:T(8,128)(2,1)} fusion(bf16[512,2,8,64]{3,2,1,0:T(8,128)(2,1)S(1)} %copy-done.2, bf16[512,2,64,128]{3,2,1,0:T(8,128)(2,1)} %bitcast.98, pred[512,2]{1,0:T(8,128)(4,1)S(1)} %get-tuple-element.153), kind=kOutput, calls=%fused_computation.8.clone.1 | convolution fusion | flops 143654912 | bytes 19923968 | tf_op jit(solution)/shard_map/while/body/eval_jaxpr/njar,njrs->njas/dot_general | solution.py:17
  122.1 3.0 copy.111
  125.2 6.6 %copy.112 = bf16[512,2,16,64]{3,2,1,0:T(8,128)(2,1)} copy(bf16[512,2,16,64]{0,3,2,1:T(8,128)(2,1)S(1)} %bitcast.99) | data formatting | bytes 4194304 | tf_op jit(solution)/shard_map/while/body/eval_jaxpr/reshape | solution.py:18
  131.8 0.2 reshape.185
  132.0 4.0 %gather_fusion.2 = bf16[1024,512]{1,0:T(8,128)(2,1)S(1)} fusion(bf16[250,512]{1,0:T(8,128)(2,1)S(1)} %copy-done.1, s32[1024]{0:T(1024)S(1)} %broadcast_clamp_fusion.8), kind=kCustom, calls=%fused_computation.1.clone.clone.1 | custom fusion | bytes 2101248 | tf_op jit(solution)/shard_map/while/body/eval_jaxpr/jit(_take)/gather | solution.py:19
  135.9 0.4 reshape.186
  136.4 1.5 copy.113
  137.9 0.1 copy.114
  138.1 3.3 %copy.115 = bf16[512,2,64,8]{2,3,1,0:T(8,128)(2,1)} copy(bf16[512,2,64,8]{0,3,2,1:T(8,128)(2,1)S(1)} %select_bitcast_fusion.2) | data formatting | bytes 2097152 | tf_op jit(solution)/shard_map/while/body/eval_jaxpr/reshape | solution.py:19
  141.4 0.1 fusion.25
  141.5 5.3 %multiply_reduce_fusion.2 = bf16[512,16,8]{1,2,0:T(8,128)(2,1)S(1)} fusion(bf16[512,2,16,64]{3,2,1,0:T(8,128)(2,1)} %copy.112, bf16[512,2,64,8]{2,3,1,0:T(8,128)(2,1)} %copy.115, f32[512,2]{1,0:T(8,128)S(1)} %fusion.25), kind=kOutput, calls=%fused_computation.7.clone.1 | convolution fusion | flops 16973824 | bytes 3280896 | tf_op jit(solution)/shard_map/while/body/eval_jaxpr/njps,njsc->njpc/dot_general | solution.py:20
  146.8 0.8 copy.116
  147.9 0.7 copy-done.4
  148.5 0.5 broadcast.56
  149.1 1.8 reduce.5
  150.8 0.8 reshape.163
  151.6 3.4 %all-to-all-start.2 = ((bf16[8,2,8192]{2,1,0:T(2,128)(2,1)}), bf16[8,2,8192]{2,1,0:T(2,128)(2,1)S(1)}, u32[]{:S(2)}, u32[]{:S(2)}) async-start(bf16[8,2,8192]{2,1,0:T(2,128)(2,1)} %reshape.163), calls=%async_computation.2 | async-start | bytes 524288 | tf_op jit(solution)/shard_map/all_to_all | solution.py:44
  155.1 1.1 copy.90
  156.2 5.7 %all-to-all-done.2 = bf16[8,2,8192]{2,1,0:T(2,128)(2,1)S(1)} async-done(((bf16[8,2,8192]{2,1,0:T(2,128)(2,1)}), bf16[8,2,8192]{2,1,0:T(2,128)(2,1)S(1)}, u32[]{:S(2)}, u32[]{:S(2)}) %all-to-all-start.2) | async-done | bytes 262176 | tf_op jit(solution)/shard_map/all_to_all | solution.py:44
  161.9 0.3 reshape.164
  162.2 0.2 copy.85
  162.4 0.7 convolution_bitcast_fusion
  163.1 2.3 copy.87
  165.4 0.9 copy.88
  166.2 139.4 %reduce-scatter.2.cloned.1.call-done = f32[128,256]{1,0:T(8,128)} async-done(((f32[4096,256]{1,0:T(8,128)}), f32[128,256]{1,0:T(8,128)}) %reduce-scatter.2.cloned.1.call-update) | async-done | bytes 131088 | tf_op jit(solution)/shard_map/reduce_scatter | solution.py:58
  (47 shorter events, 1.3 us)
Async XLA Ops:
  7.2 9.8 %all-to-all-start.1 = ((s32[128,8,1]{0,2,1:T(1,128)}), s32[128,8,1]{0,2,1:T(1,128)S(1)}, u32[]{:S(2)}, u32[]{:S(2)}) async-start(s32[128,8,1]{0,2,1:T(1,128)} %bitcast.113), calls=%async_computation.1 | async-start | bytes 8192 | tf_op jit(solution)/shard_map/all_to_all | solution.py:30
  16.9 8.1 %all-to-all-start = ((s32[128,8,3,2]{0,3,2,1:T(2,128)}), s32[128,8,3,2]{0,3,2,1:T(2,128)S(1)}, u32[]{:S(2)}, u32[]{:S(2)}) async-start(s32[128,8,3,2]{0,3,2,1:T(2,128)} %param.10), calls=%async_computation | async-start | bytes 49152 | tf_op jit(solution)/shard_map/all_to_all | solution.py:29
  25.0 1.0 copy-start
  35.5 15.8 %copy-start.2 = (bf16[512,2,8,64]{3,2,1,0:T(8,128)(2,1)S(1)}, bf16[512,2,8,64]{3,2,1,0:T(8,128)(2,1)}, u32[]{:S(2)}) copy-start(bf16[512,2,8,64]{3,2,1,0:T(8,128)(2,1)} %copy.110) | copy-start | bytes 3145732 | tf_op jit(solution)/shard_map/while
  63.4 6.8 %copy-start.1 = (bf16[250,512]{1,0:T(8,128)(2,1)S(1)}, bf16[250,512]{1,0:T(8,128)(2,1)}, u32[]{:S(2)}) copy-start(bf16[250,512]{1,0:T(8,128)(2,1)} %get-tuple-element.177) | copy-start | bytes 768004 | tf_op jit(solution)/shard_map/while
  79.8 6.3 %copy-start.3 = (bf16[2,512,128]{2,1,0:T(8,128)(2,1)S(1)}, bf16[2,512,128]{2,1,0:T(8,128)(2,1)}, u32[]{:S(2)}) copy-start(bf16[2,512,128]{2,1,0:T(8,128)(2,1)} %get-tuple-element.165) | copy-start | bytes 786436 | tf_op jit(solution)/shard_map/while
  86.1 0.7 copy-start.4
  86.8 0.9 copy-start
  97.2 15.8 %copy-start.2 = (bf16[512,2,8,64]{3,2,1,0:T(8,128)(2,1)S(1)}, bf16[512,2,8,64]{3,2,1,0:T(8,128)(2,1)}, u32[]{:S(2)}) copy-start(bf16[512,2,8,64]{3,2,1,0:T(8,128)(2,1)} %copy.110) | copy-start | bytes 3145732 | tf_op jit(solution)/shard_map/while
  125.1 6.8 %copy-start.1 = (bf16[250,512]{1,0:T(8,128)(2,1)S(1)}, bf16[250,512]{1,0:T(8,128)(2,1)}, u32[]{:S(2)}) copy-start(bf16[250,512]{1,0:T(8,128)(2,1)} %get-tuple-element.177) | copy-start | bytes 768004 | tf_op jit(solution)/shard_map/while
  141.5 6.3 %copy-start.3 = (bf16[2,512,128]{2,1,0:T(8,128)(2,1)S(1)}, bf16[2,512,128]{2,1,0:T(8,128)(2,1)}, u32[]{:S(2)}) copy-start(bf16[2,512,128]{2,1,0:T(8,128)(2,1)} %get-tuple-element.165) | copy-start | bytes 786436 | tf_op jit(solution)/shard_map/while
  147.8 0.7 copy-start.4
  151.6 10.3 %all-to-all-start.2 = ((bf16[8,2,8192]{2,1,0:T(2,128)(2,1)}), bf16[8,2,8192]{2,1,0:T(2,128)(2,1)S(1)}, u32[]{:S(2)}, u32[]{:S(2)}) async-start(bf16[8,2,8192]{2,1,0:T(2,128)(2,1)} %reshape.163), calls=%async_computation.2 | async-start | bytes 524288 | tf_op jit(solution)/shard_map/all_to_all | solution.py:44
  155.0 150.7 %reduce-scatter.2.cloned.1.call-start = ((), (), s32[]{:S(2)}) async-start(), calls=%async_computation.4 | async-start | bytes 4325376 | tf_op jit(solution)/shard_map/reduce_scatter | solution.py:58
Sparse Core Ops, SparseCore 0:
  165.5 140.1 reduce-scatter.1
where the time goes:
time: 313 us
  waiting for transfers between devices  154 us (49%)
  local copies, waits for them, and re-layouts  98.9 us (32%)
  matrix products  29.6 us (9%)
  between operations  14.1 us (5%)
  starting transfers between devices  12 us (4%)
  other arithmetic  3.16 us (1%)
    reduce_scatter x1, waiting for transfers between devices, body(): lax.psum_scatter(arranged, ('dp', 'table'), scatter_dimension=0, tiled=True)  139 us
    gather x2, local copies, waits for them, and re-layouts, build_rows(): centre = jnp.take(middle, wanted[:, 1, :], axis=0)  31.5 us
    dot_general x2, matrix products, build_rows(): jnp.einsum('njar,njrs->njas', head, centre, preferred_element_type=jnp.fl...  18.3 us
    reshape x2, local copies, waits for them, and re-layouts, build_rows(): prefix = prefix.astype(jnp.bfloat16).reshape(block, BAG, D1 * D2, RANK)  13.3 us
    gather x6, local copies, waits for them, and re-layouts, build_rows(): tail = jnp.take(last, wanted[:, 2, :], axis=0).reshape(block, BAG, RANK, D3)  11.7 us
    gather x6, local copies, waits for them, and re-layouts, build_rows(): jnp.take(first, wanted[:, 0, :], axis=0).reshape(block, BAG, D1, RANK)  11.7 us
    dot_general x2, matrix products, build_rows(): jnp.einsum('njps,njsc->njpc', prefix, tail, preferred_element_type=jnp.fl...  10.6 us
    reshape x2, local copies, waits for them, and re-layouts, build_rows(): tail = jnp.take(last, wanted[:, 2, :], axis=0).reshape(block, BAG, RANK, D3)  6.57 us
  transfers between devices with their start and end apart: 4, of which 4 were waited for; matrix products, arithmetic and copies ran while one was open for 1% of the time, Pallas kernels for 0%

commit v1 on v0

v1 whole, which is shorter than its diff:
```python
import functools

import jax
import jax.numpy as jnp
from jax import lax
from jax.experimental import pallas as pl
from jax.experimental.pallas import tpu as pltpu
from jax.sharding import PartitionSpec as P

D1 = 8
D2 = 2
D3 = 8
RANK = 64
BAG = 2
LANES = 128
WIDTH = D1 * D2 * D3
SPAN = D1 * LANES
PAD = 256
UNROLL = 2
MESH = pl.DeviceIdType.MESH
F32 = jnp.float32
BF16 = jnp.bfloat16


def iota(shape, dim):
    return lax.broadcasted_iota(jnp.int32, shape, dim)


def spread_tables(first, last, firstx, lastx):
    ncore, wide = first.shape
    firstx[...] = jnp.zeros_like(firstx)
    lastx[...] = jnp.zeros_like(lastx)
    row = iota((wide, LANES), 0)
    lane = lax.rem(iota((wide, LANES), 1), RANK)
    for a in range(D1):
        span = slice(a * LANES, (a + 1) * LANES)
        pick = (row == a * RANK + lane).astype(F32).astype(BF16)
        firstx[0:ncore, span] = jnp.dot(first[...], pick, preferred_element_type=F32).astype(BF16)
        pick = (row == lane * D3 + a).astype(F32).astype(BF16)
        lastx[0:ncore, span] = jnp.dot(last[...], pick, preferred_element_type=F32).astype(BF16)


def gather_ends(tile, firstx, lastx, heads, tails):
    block = tile.shape[1]
    columns = jnp.transpose(tile)
    slices = iota((block, PAD), 1)
    for j in range(BAG):
        live = columns[:, 6:7] > j
        p = jnp.where(live, columns[:, j : j + 1], -1)
        u = columns[:, 4 + j : 5 + j]
        hot = (p == slices).astype(F32).astype(BF16)
        heads[j] = jnp.dot(hot, firstx[...], preferred_element_type=F32)
        hot = (u == slices).astype(F32).astype(BF16)
        tails[j] = jnp.dot(hot, lastx[...], preferred_element_type=F32)


def lookups(smem, slot, middle, heads, tails, spread, block):
    row16, lane16 = iota((16, LANES), 0), iota((16, LANES), 1)
    half = lane16 // RANK
    masks = []
    for kt in range(4):
        keep = (lax.rem(row16, 8) == 2 * kt + half).astype(F32).astype(BF16)
        masks.append(jnp.concatenate([keep] * 4, axis=0))
    sides = []
    for b in range(D2):
        keep = (half == b).astype(F32).astype(BF16)
        sides.append(jnp.concatenate([keep] * 4, axis=0))
    diagonal = (iota((8, LANES), 0) == lax.rem(iota((8, LANES), 1), 8)).astype(F32)
    diagonal = jnp.concatenate([diagonal] * D1, axis=0)

    def step(g, carry):
        base = pl.multiple_of(g * 16, 16)
        parts = []
        for h in range(2):
            at = base + 8 * h
            rows = pl.ds(pl.multiple_of(at, 8), 8)
            total = None
            for j in range(BAG):
                head = jnp.concatenate(
                    [heads[j, rows, a * LANES : (a + 1) * LANES] for a in range(D1)], axis=0
                ).astype(BF16)
                head = jnp.concatenate([head * mask for mask in masks], axis=1)
                centre = jnp.concatenate(
                    [middle[smem[slot, 2 + j, at + i]] for i in range(8)], axis=0
                )
                prefix = jnp.dot(head, centre, preferred_element_type=F32).astype(BF16)
                tail = jnp.concatenate(
                    [tails[j, rows, c * LANES : (c + 1) * LANES] for c in range(D3)], axis=0
                ).astype(BF16)
                tail = jnp.concatenate([tail * side for side in sides], axis=0)
                out = lax.dot_general(
                    prefix, tail, (((1,), (1,)), ((), ())), preferred_element_type=F32
                )
                total = out if total is None else total + out
            parts.append(total * diagonal)
        for a in range(D1):
            both = jnp.concatenate([part[a * 8 : (a + 1) * 8] for part in parts], axis=0)
            spread[pl.ds(base, 16), a * LANES : (a + 1) * LANES] = both.astype(BF16)
        return carry

    lax.fori_loop(0, block // 16, step, 0, unroll=UNROLL)


def kernel(nd, nt, tiles, first, middle, last, grad, pooled, wg,
           ids, smem, mid, grads, rows, sib, firstx, lastx, heads, tails, spread, fold, part, partin,
           mid_sem, smem_sem, ids_ss, ids_rs, grad_ss, grad_rs, pool_ss, pool_rs, sib_ss, sib_rs,
           part_ss, part_rs):
    d, t = lax.axis_index("dp"), lax.axis_index("table")
    core = lax.rem(t, 2)
    pair = t - core
    other = pair + 1 - core
    block = grad.shape[0]
    half = grads.shape[2]
    cols = wg.shape[1]
    per = nd // 2

    load = pltpu.make_async_copy(middle, mid, mid_sem)
    load.start()
    pltpu.make_async_copy(tiles.at[t], smem.at[0], smem_sem.at[0]).start()

    barrier = pltpu.get_barrier_semaphore()
    for k in range(1, nt):
        pl.semaphore_signal(barrier, inc=1, device_id=(d, lax.rem(t + k, nt)), device_id_type=MESH)
    for k in range(1, nd):
        for e in range(2):
            pl.semaphore_signal(
                barrier, inc=1, device_id=(lax.rem(d + k, nd), pair + e), device_id_type=MESH
            )
    pl.semaphore_wait(barrier, nt - 1 + 2 * (nd - 1))

    def send_ids(k):
        peer = lax.rem(t + k, nt)
        return pltpu.make_async_remote_copy(
            tiles.at[peer], ids.at[t], ids_ss.at[k], ids_rs.at[k],
            device_id=(d, peer), device_id_type=MESH)

    def send_grad(k):
        peer = lax.rem(t + k, nt)
        mine = pl.ds(pl.multiple_of(lax.rem(peer, 2) * half, LANES), half)
        return pltpu.make_async_remote_copy(
            grad.at[:, mine], grads.at[t], grad_ss.at[k], grad_rs.at[k],
            device_id=(d, peer), device_id_type=MESH)

    def send_pooled(k):
        peer = lax.rem(t - k + nt, nt)
        return pltpu.make_async_remote_copy(
            rows.at[peer], pooled.at[:, pl.ds(pl.multiple_of(t * WIDTH, LANES), WIDTH)],
            pool_ss.at[k], pool_rs.at[k], device_id=(d, peer), device_id_type=MESH)

    def send_sib(k):
        peer = lax.rem(t - k + nt, nt)
        return pltpu.make_async_remote_copy(
            rows.at[peer], sib.at[peer], sib_ss.at[peer], sib_rs.at[peer],
            device_id=(d, other), device_id_type=MESH)

    for k in range(1, nt):
        send_ids(k).start()
    for k in range(1, nt):
        send_grad(k).start()
    ids[t] = tiles[t]
    grads[t] = grad[:, pl.ds(pl.multiple_of(core * half, LANES), half)]

    spread_tables(first, last, firstx, lastx)
    fold[...] = (iota(fold.shape, 0) // 8 == iota(fold.shape, 1)).astype(F32).astype(BF16)
    load.wait()

    def chunk(k, carry):
        s = lax.rem(t - k + nt, nt)
        slot = lax.rem(k, 2)
        pltpu.make_async_copy(ids.at[s], smem.at[slot], smem_sem.at[slot]).wait()

        @pl.when(k + 1 < nt)
        def _():
            after = lax.rem(t - k - 1 + nt, nt)
            pltpu.make_async_remote_copy(
                ids.at[after], ids.at[after], ids_ss.at[k + 1], ids_rs.at[k + 1],
                device_id=(d, other), device_id_type=MESH).wait_recv()
            pltpu.make_async_copy(ids.at[after], smem.at[1 - slot], smem_sem.at[1 - slot]).start()

        gather_ends(ids[s], firstx, lastx, heads, tails)
        lookups(smem, slot, mid, heads, tails, spread, block)
        done = jnp.dot(spread[...], fold[...], preferred_element_type=F32).astype(BF16)
        rows[s] = done
        send_sib(k).start()

        @pl.when(k > 0)
        def _():
            send_pooled(k).start()

        @pl.when(k == 0)
        def _():
            pooled[:, pl.ds(pl.multiple_of(t * WIDTH, LANES), WIDTH)] = done

        return carry

    lax.fori_loop(0, nt, chunk, 0)

    for k in range(1, nt):
        s = lax.rem(t - k + nt, nt)
        pltpu.make_async_remote_copy(
            grads.at[s], grads.at[s], grad_ss.at[k], grad_rs.at[k],
            device_id=(d, other), device_id_type=MESH).wait_recv()
    for s in range(nt):
        pltpu.make_async_remote_copy(
            sib.at[s], sib.at[s], sib_ss.at[s], sib_rs.at[s],
            device_id=(d, other), device_id_type=MESH).wait_recv()

    group = nt * block

    def partial(mine, q):
        left = rows if mine else sib
        return lax.dot_general(
            left[...].reshape(group, WIDTH), grads[:, :, q * cols : (q + 1) * cols].reshape(group, cols),
            (((0,), (0,)), ((), ())), preferred_element_type=F32).astype(BF16)

    def send_part(mine, q):
        target = core * per + q
        return pltpu.make_async_remote_copy(
            part.at[mine, q], partin.at[d], part_ss.at[mine, q], part_rs.at[d],
            device_id=(target, t if mine else other), device_id_type=MESH)

    for mine in (1, 0):
        for q in range(per):
            part[mine, q] = partial(mine, q)
            if mine:
                @pl.when(core * per + q != d)
                def _():
                    send_part(mine, q).start()

                @pl.when(core * per + q == d)
                def _():
                    partin[d] = part[mine, q]
            else:
                send_part(mine, q).start()

    for k in range(1, nt):
        send_ids(k).wait_send()
        send_grad(k).wait_send()
        send_pooled(k).wait_send()
        s = lax.rem(t + k, nt)
        pltpu.make_async_remote_copy(
            rows.at[s], pooled.at[:, pl.ds(pl.multiple_of(s * WIDTH, LANES), WIDTH)],
            pool_ss.at[k], pool_rs.at[k], device_id=(d, other), device_id_type=MESH).wait_recv()
    for k in range(nt):
        send_sib(k).wait_send()

    source = d // per
    for k in range(nd):
        @pl.when(jnp.logical_or(source != core, k != d))
        def _():
            pltpu.make_async_remote_copy(
                partin.at[k], partin.at[k], part_ss.at[0, 0], part_rs.at[k],
                device_id=(d, other), device_id_type=MESH).wait_recv()
    total = partin[0].astype(F32)
    for k in range(1, nd):
        total = total + partin[k].astype(F32)
    wg[...] = total
    for mine in (1, 0):
        for q in range(per):
            if mine:
                @pl.when(core * per + q != d)
                def _():
                    send_part(mine, q).wait_send()
            else:
                send_part(mine, q).wait_send()


def body(core_ids, bag_lengths, first_core, middle_core, last_core, grad_hidden):
    nd, nt = lax.axis_size("dp"), lax.axis_size("table")
    block, hidden = grad_hidden.shape
    ncore = middle_core.shape[1]
    tiles = jnp.concatenate(
        [
            jnp.transpose(core_ids, (1, 2, 3, 0)).reshape(nt, 3 * BAG, block),
            jnp.transpose(bag_lengths)[:, None, :],
            jnp.zeros((nt, 1, block), jnp.int32),
        ],
        axis=1,
    )
    cols = hidden // nd
    half = hidden // 2
    vmem = pl.BlockSpec(memory_space=pltpu.VMEM)
    dma = pltpu.SemaphoreType.DMA
    return pl.pallas_call(
        functools.partial(kernel, nd, nt),
        out_shape=(
            jax.ShapeDtypeStruct((block, nt * WIDTH), BF16),
            jax.ShapeDtypeStruct((WIDTH, cols), F32),
        ),
        in_specs=[vmem, vmem, pl.BlockSpec(memory_space=pl.ANY), vmem, vmem],
        out_specs=(vmem, vmem),
        scratch_shapes=[
            pltpu.VMEM((nt, 8, block), jnp.int32),
            pltpu.SMEM((2, 8, block), jnp.int32),
            pltpu.VMEM((ncore, RANK, D2 * RANK), BF16),
            pltpu.VMEM((nt, block, half), BF16),
            pltpu.VMEM((nt, block, WIDTH), BF16),
            pltpu.VMEM((nt, block, WIDTH), BF16),
            pltpu.VMEM((PAD, SPAN), BF16),
            pltpu.VMEM((PAD, SPAN), BF16),
            pltpu.VMEM((BAG, block, SPAN), F32),
            pltpu.VMEM((BAG, block, SPAN), F32),
            pltpu.VMEM((block, SPAN), BF16),
            pltpu.VMEM((SPAN, WIDTH), BF16),
            pltpu.VMEM((2, nd // 2, WIDTH, cols), BF16),
            pltpu.VMEM((nd, WIDTH, cols), BF16),
            dma, dma((2,)),
            dma((nt,)), dma((nt,)), dma((nt,)), dma((nt,)), dma((nt,)), dma((nt,)),
            dma((nt,)), dma((nt,)), dma((2, nd // 2)), dma((nd,)),
        ],
        compiler_params=pltpu.CompilerParams(
            collective_id=0, has_side_effects=True, vmem_limit_bytes=48 * 1024 * 1024
        ),
        cost_estimate=pl.CostEstimate(flops=2 * 10**9, bytes_accessed=6 * 10**6, transcendentals=0),
    )(tiles, first_core[0], middle_core[0], last_core[0], grad_hidden)


def solution(mesh):
    placed = (
        P(("dp", "table"), None, None, None),
        P(("dp", "table"), None),
        P("table", None, None),
        P("table", None, None, None),
        P("table", None, None),
        P(("dp", "table"), None),
    )
    return jax.shard_map(
        body,
        mesh=mesh,
        in_specs=placed,
        out_specs=(P(("dp", "table"), None), P("table", "dp")),
        check_vma=False,
    )
```

time: 313 us -> 49.2 us (0.16)
  the two profiles are of different devices: /device:TPU:0 before, /device:TPU:1 now
where the time goes in v1:
time: 49.2 us; the launch traced here: 48.8 us
  Pallas kernels  40.2 us (82%)
  local copies, waits for them, and re-layouts  7.19 us (15%)
  other arithmetic  0.76 us (2%)
  between operations  0.64 us (1%)
    pallas_call x1, Pallas kernels, body(): pl.pallas_call(functools.partial(kernel, nd, nt), out_shape=(jax.ShapeDty...  40.2 us
    unnamed x11, local copies, waits for them, and re-layouts  7.11 us

profile of v1, /device:TPU:1, one launch (start us, length us, event | category | flops | bytes accessed | tf_op | source)
XLA Modules:
  0.0 48.8 jit_solution(13992143375866255275)
XLA Ops:
  0.6 0.1 pad.2.clone
  0.7 0.7 %copy.8 = s32[128,8,3,2]{0,1,3,2:T(8,128)S(1)} copy(s32[128,8,3,2]{0,3,2,1:T(2,128)} %param.6) | data formatting | bytes 49152 | tf_op args[0]
  1.5 0.8 %add_add_fusion.tiles = s32[8,8,128]{2,1,0:T(8,128)S(1)} fusion(s32[8,1,128]{2,1,0:T(1,128)} %bitcast.14, s32[8,6,128]{2,1,0:T(8,128)S(1)} %copy.9, s32[8]{0:T(128)S(1)} %pad.2.clone), kind=kLoop, calls=%fused_computation | loop fusion | flops 16384 | bytes 61472 | tf_op jit(solution)/shard_map/concatenate | solution.py:272
  2.2 0.0 copy-start
  2.2 2.2 %copy-done = bf16[1,250,64,128]{3,2,1,0:T(8,128)(2,1)S(1)} copy-done((bf16[1,250,64,128]{3,2,1,0:T(8,128)(2,1)S(1)}, bf16[1,250,64,128]{3,2,1,0:T(8,128)(2,1)}, u32[]{:S(2)}) %copy-start) | copy-done | bytes 4096024
  4.4 0.0 copy-start.1
  4.4 0.9 %copy-done.1 = bf16[1,250,512]{2,1,0:T(8,128)(2,1)S(1)} copy-done((bf16[1,250,512]{2,1,0:T(8,128)(2,1)S(1)}, bf16[1,250,512]{2,1,0:T(8,128)(2,1)}, u32[]{:S(2)}) %copy-start.1) | copy-done | bytes 256024
  5.3 0.0 copy-start.2
  5.3 0.9 %copy-done.2 = bf16[1,250,512]{2,1,0:T(8,128)(2,1)S(1)} copy-done((bf16[1,250,512]{2,1,0:T(8,128)(2,1)S(1)}, bf16[1,250,512]{2,1,0:T(8,128)(2,1)}, u32[]{:S(2)}) %copy-start.2) | copy-done | bytes 256024
  6.3 0.0 copy-start.3
  6.3 0.9 %copy-done.3 = bf16[128,1024]{1,0:T(8,128)(2,1)S(1)} copy-done((bf16[128,1024]{1,0:T(8,128)(2,1)S(1)}, bf16[128,1024]{1,0:T(8,128)(2,1)}, u32[]{:S(2)}) %copy-start.3) | copy-done | bytes 262168
  7.2 40.2 %shard_map.77 = (bf16[128,1024]{1,0:T(8,128)(2,1)S(1)}, f32[128,256]{1,0:T(8,128)S(1)}) custom-call(s32[8,8,128]{2,1,0:T(8,128)S(1)} %add_add_fusion.tiles, bf16[250,512]{1,0:T(8,128)(2,1)S(1)} %bitcast.11, bf16[250,64,128]{2,1,0:T(8,128)(2,1)S(1)} %bitcast.10, bf16[250,512]{1,0:T(8,128)(2,1)S(1)} %bitcast.12, bf16[128,1024]{1,0:T(8,128)(2,1)S(1)} %copy-done.3), custom_call_target="tpu_custom_call" | custom-call | flops 2000000000 | bytes 6000000 | tf_op jit(solution)/shard_map/pallas_call | solution.py:284
  47.5 0.7 %copy.12 = bf16[128,1024]{1,0:T(8,128)(2,1)} copy(bf16[128,1024]{1,0:T(8,128)(2,1)S(1)} %get-tuple-element.4) | data formatting | bytes 524288
  48.2 0.7 %copy.13 = f32[128,256]{1,0:T(8,128)} copy(f32[128,256]{1,0:T(8,128)S(1)} %get-tuple-element.5) | data formatting | bytes 262144
  (1 shorter events, 0.0 us)
Async XLA Ops:
  2.2 2.2 %copy-start = (bf16[1,250,64,128]{3,2,1,0:T(8,128)(2,1)S(1)}, bf16[1,250,64,128]{3,2,1,0:T(8,128)(2,1)}, u32[]{:S(2)}) copy-start(bf16[1,250,64,128]{3,2,1,0:T(8,128)(2,1)} %param.9) | copy-start | bytes 12288004
  4.4 0.9 %copy-start.1 = (bf16[1,250,512]{2,1,0:T(8,128)(2,1)S(1)}, bf16[1,250,512]{2,1,0:T(8,128)(2,1)}, u32[]{:S(2)}) copy-start(bf16[1,250,512]{2,1,0:T(8,128)(2,1)} %param.8) | copy-start | bytes 768004
  5.3 0.9 %copy-start.2 = (bf16[1,250,512]{2,1,0:T(8,128)(2,1)S(1)}, bf16[1,250,512]{2,1,0:T(8,128)(2,1)}, u32[]{:S(2)}) copy-start(bf16[1,250,512]{2,1,0:T(8,128)(2,1)} %param.10) | copy-start | bytes 768004
  6.3 0.9 %copy-start.3 = (bf16[128,1024]{1,0:T(8,128)(2,1)S(1)}, bf16[128,1024]{1,0:T(8,128)(2,1)}, u32[]{:S(2)}) copy-start(bf16[128,1024]{1,0:T(8,128)(2,1)} %grad.1) | copy-start | bytes 786436

commit v2 on v1

v2 whole, which is shorter than its diff:
```python
import functools

import jax
import jax.numpy as jnp
from jax import lax
from jax.experimental import pallas as pl
from jax.experimental.pallas import tpu as pltpu
from jax.sharding import PartitionSpec as P

D1 = 8
D2 = 2
D3 = 8
RANK = 64
BAG = 2
LANES = 128
WIDTH = D1 * D2 * D3
SPAN = D1 * LANES
LAG = 2
MESH = pl.DeviceIdType.MESH
F32 = jnp.float32
BF16 = jnp.bfloat16


def iota(shape, dim):
    return lax.broadcasted_iota(jnp.int32, shape, dim)


def spread_tables(first, last, firstx, wide, lastx):
    ncore, length = first.shape
    row = iota((length, LANES), 0)
    lane = lax.rem(iota((length, LANES), 1), RANK)
    half = iota((ncore, LANES), 1) // RANK
    wide[0 : firstx.shape[0] * D1] = jnp.zeros((firstx.shape[0] * D1, LANES), F32)
    for a in range(D1):
        pick = (row == a * RANK + lane).astype(F32).astype(BF16)
        wide[pl.ds(a, ncore, stride=D1), :] = jnp.dot(first[...], pick, preferred_element_type=F32)
    firstx[...] = wide[0 : firstx.shape[0] * D1].reshape(firstx.shape)
    for c in range(D3):
        pick = (row == lane * D3 + c).astype(F32).astype(BF16)
        found = jnp.dot(last[...], pick, preferred_element_type=F32)
        for b in range(D2):
            wide[pl.ds(b * D3 + c, ncore, stride=D2 * D3), :] = jnp.where(half == b, found, 0.0)
    lastx[...] = wide[...].reshape(lastx.shape).astype(BF16)


def heads_of(smem, slot, firstx, middle, at):
    upper = (iota((8, LANES), 1) >= RANK).astype(F32)
    lower = 1.0 - upper
    zero = jnp.zeros((16, LANES), BF16)
    groups = []
    for g in range(2):
        lefts, rights = [], []
        for j in range(BAG):
            heads, centres = [], []
            for i in range(4):
                n = at + g * 4 + i
                heads.append(firstx[smem[slot, j, n]] * (upper if i % 2 else lower))
                centres.append(middle[smem[slot, 2 + j, n]])
            top = jnp.concatenate(heads[:2], axis=0).astype(BF16)
            low = jnp.concatenate(heads[2:], axis=0).astype(BF16)
            lefts.append(jnp.concatenate([top, zero], axis=1))
            lefts.append(jnp.concatenate([zero, low], axis=1))
            rights.append(jnp.concatenate(centres, axis=0))
        both = jnp.dot(jnp.concatenate(lefts, axis=0), jnp.concatenate(rights, axis=1),
                       preferred_element_type=F32)
        groups.append(jnp.concatenate(
            [both[j * 32 : (j + 1) * 32, j * LANES : (j + 1) * LANES] for j in range(BAG)], axis=1
        ).astype(BF16))
    return jnp.concatenate(groups, axis=0)


def tails_of(smem, slot, prefix, lastx, at):
    sides = []
    for j in range(BAG):
        tails = []
        for i in range(8):
            tails.append(lastx[smem[slot, 4 + j, at + i]])
        sides.append(jnp.concatenate(tails, axis=0))
    out = lax.dot_general(prefix, jnp.concatenate(sides, axis=1), (((1,), (1,)), ((), ())),
                          preferred_element_type=F32)
    owner = iota((8, LANES), 1) // 16
    total = out[0:8]
    for i in range(1, 8):
        total = jnp.where(owner == i, out[i * 8 : (i + 1) * 8], total)
    return total


def lookups(smem, slot, firstx, middle, lastx, found, block):
    prefixes = {}
    count = block // 8
    for g in range(count + LAG):
        if g < count:
            prefixes[g] = heads_of(smem, slot, firstx, middle, g * 8)
        if g >= LAG:
            h = g - LAG
            found[h * 8 : (h + 1) * 8, :] = tails_of(smem, slot, prefixes.pop(h), lastx, h * 8)


def unfold(found, ordered, block):
    count = block // 8
    values = found[...].astype(BF16)
    row, col = iota((LANES, SPAN), 0), iota((LANES, SPAN), 1)
    copies = jnp.logical_and(row // 16 == col // LANES, lax.rem(row, 16) == lax.rem(col, 16))
    copied = jnp.dot(values, copies.astype(F32).astype(BF16), preferred_element_type=F32)
    row, col = iota((block, LANES), 0), iota((block, LANES), 1)
    keep = (lax.rem(row, 8) == col // 16).astype(F32)
    kept = jnp.concatenate(
        [copied[:, i * LANES : (i + 1) * LANES] * keep for i in range(8)], axis=1).astype(BF16)
    add = (iota((count, block), 1) // 8 == iota((count, block), 0)).astype(F32).astype(BF16)
    sums = jnp.dot(add, kept, preferred_element_type=F32)
    for i in range(8):
        ordered[pl.ds(i, count, stride=8), :] = sums[:, i * LANES : (i + 1) * LANES]
    return ordered[...].astype(BF16)


def kernel(nd, nt, core_ids, lengths, first, middle, last, grad, pooled, wg,
           raw_ids, raw_lengths, tiles, ids, smem, mid, ends, grads, rows, sib, firstx, wide, lastx, found, ordered, part, partin,
           raw_sem, mid_sem, end_sem, own_sem, smem_sem, ids_ss, ids_rs, grad_ss, grad_rs, pool_ss, pool_rs, sib_ss, sib_rs,
           part_ss, part_rs):
    d, t = lax.axis_index("dp"), lax.axis_index("table")
    core = lax.rem(t, 2)
    pair = t - core
    other = pair + 1 - core
    block = grad.shape[0]
    ncore = middle.shape[0]
    half = grads.shape[2]
    cols = wg.shape[1]
    per = nd // 2

    load = pltpu.make_async_copy(middle, mid, mid_sem)
    loads = [pltpu.make_async_copy(ref, ends.at[k], end_sem.at[k]) for k, ref in enumerate((first, last))]
    raws = [pltpu.make_async_copy(core_ids, raw_ids, raw_sem.at[0]),
            pltpu.make_async_copy(lengths, raw_lengths, raw_sem.at[1])]
    for copy in raws + loads:
        copy.start()
    load.start()

    barrier = pltpu.get_barrier_semaphore()
    for k in range(1, nt):
        pl.semaphore_signal(barrier, inc=1, device_id=(d, lax.rem(t + k, nt)), device_id_type=MESH)
    for k in range(1, nd):
        for e in range(2):
            pl.semaphore_signal(
                barrier, inc=1, device_id=(lax.rem(d + k, nd), pair + e), device_id_type=MESH
            )
    own = pltpu.make_async_copy(
        grad.at[:, pl.ds(pl.multiple_of(core * half, LANES), half)], grads.at[t], own_sem)
    own.start()
    for copy in raws:
        copy.wait()
    slots = iota((BAG, block), 0)
    for k in range(nt):
        live = slots < raw_lengths[k : k + 1, :]
        tiles[k, 0:BAG] = jnp.where(live, raw_ids[k, 0], ncore)
        tiles[k, BAG : 2 * BAG] = raw_ids[k, 1]
        tiles[k, 2 * BAG : 3 * BAG] = raw_ids[k, 2]
        tiles[k, 3 * BAG :] = jnp.zeros((8 - 3 * BAG, block), jnp.int32)
    pltpu.make_async_copy(tiles.at[t], smem.at[0], smem_sem.at[0]).start()
    for copy in loads:
        copy.wait()
    spread_tables(ends.at[0], ends.at[1], firstx, wide, lastx)
    pl.semaphore_wait(barrier, nt - 1 + 2 * (nd - 1))

    def send_ids(k):
        peer = lax.rem(t + k, nt)
        return pltpu.make_async_remote_copy(
            tiles.at[peer], ids.at[t], ids_ss.at[k], ids_rs.at[k],
            device_id=(d, peer), device_id_type=MESH)

    def send_grad(k):
        peer = lax.rem(t + k, nt)
        mine = pl.ds(pl.multiple_of(lax.rem(peer, 2) * half, LANES), half)
        return pltpu.make_async_remote_copy(
            grad.at[:, mine], grads.at[t], grad_ss.at[k], grad_rs.at[k],
            device_id=(d, peer), device_id_type=MESH)

    def send_pooled(k):
        peer = lax.rem(t - k + nt, nt)
        return pltpu.make_async_remote_copy(
            rows.at[peer], pooled.at[:, pl.ds(pl.multiple_of(t * WIDTH, LANES), WIDTH)],
            pool_ss.at[k], pool_rs.at[k], device_id=(d, peer), device_id_type=MESH)

    def send_sib(k):
        peer = lax.rem(t - k + nt, nt)
        return pltpu.make_async_remote_copy(
            rows.at[peer], sib.at[peer], sib_ss.at[peer], sib_rs.at[peer],
            device_id=(d, other), device_id_type=MESH)

    for k in range(1, nt):
        send_ids(k).start()
    for k in range(1, nt):
        send_grad(k).start()
    load.wait()

    def chunk(k, carry):
        s = lax.rem(t - k + nt, nt)
        slot = lax.rem(k, 2)
        pltpu.make_async_copy(ids.at[s], smem.at[slot], smem_sem.at[slot]).wait()

        @pl.when(k + 1 < nt)
        def _():
            after = lax.rem(t - k - 1 + nt, nt)
            pltpu.make_async_remote_copy(
                ids.at[after], ids.at[after], ids_ss.at[k + 1], ids_rs.at[k + 1],
                device_id=(d, other), device_id_type=MESH).wait_recv()
            pltpu.make_async_copy(ids.at[after], smem.at[1 - slot], smem_sem.at[1 - slot]).start()

        lookups(smem, slot, firstx, mid, lastx, found, block)
        done = unfold(found, ordered, block)
        rows[s] = done
        send_sib(k).start()

        @pl.when(k > 0)
        def _():
            send_pooled(k).start()

        @pl.when(k == 0)
        def _():
            pooled[:, pl.ds(pl.multiple_of(t * WIDTH, LANES), WIDTH)] = done

        return carry

    lax.fori_loop(0, nt, chunk, 0)
    own.wait()

    for k in range(1, nt):
        s = lax.rem(t - k + nt, nt)
        pltpu.make_async_remote_copy(
            grads.at[s], grads.at[s], grad_ss.at[k], grad_rs.at[k],
            device_id=(d, other), device_id_type=MESH).wait_recv()
    for s in range(nt):
        pltpu.make_async_remote_copy(
            sib.at[s], sib.at[s], sib_ss.at[s], sib_rs.at[s],
            device_id=(d, other), device_id_type=MESH).wait_recv()

    group = nt * block

    def partial(mine):
        left = rows if mine else sib
        return lax.dot_general(
            left[...].reshape(group, WIDTH), grads[...].reshape(group, half),
            (((0,), (0,)), ((), ())), preferred_element_type=F32).astype(BF16)

    def send_part(mine, q):
        target = core * per + q
        return pltpu.make_async_remote_copy(
            part.at[mine, q], partin.at[d], part_ss.at[mine, q], part_rs.at[d],
            device_id=(target, t if mine else other), device_id_type=MESH)

    for mine in (1, 0):
        whole = partial(mine)
        for q in range(per):
            part[mine, q] = whole[:, q * cols : (q + 1) * cols]
            if mine:
                @pl.when(core * per + q != d)
                def _():
                    send_part(mine, q).start()

                @pl.when(core * per + q == d)
                def _():
                    partin[d] = part[mine, q]
            else:
                send_part(mine, q).start()

    for k in range(1, nt):
        send_ids(k).wait_send()
        send_grad(k).wait_send()
        send_pooled(k).wait_send()
        s = lax.rem(t + k, nt)
        pltpu.make_async_remote_copy(
            rows.at[s], pooled.at[:, pl.ds(pl.multiple_of(s * WIDTH, LANES), WIDTH)],
            pool_ss.at[k], pool_rs.at[k], device_id=(d, other), device_id_type=MESH).wait_recv()
    for k in range(nt):
        send_sib(k).wait_send()

    source = d // per
    for k in range(nd):
        @pl.when(jnp.logical_or(source != core, k != d))
        def _():
            pltpu.make_async_remote_copy(
                partin.at[k], partin.at[k], part_ss.at[0, 0], part_rs.at[k],
                device_id=(d, other), device_id_type=MESH).wait_recv()
    total = partin[0].astype(F32)
    for k in range(1, nd):
        total = total + partin[k].astype(F32)
    wg[...] = total
    for mine in (1, 0):
        for q in range(per):
            if mine:
                @pl.when(core * per + q != d)
                def _():
                    send_part(mine, q).wait_send()
            else:
                send_part(mine, q).wait_send()


def body(core_ids, bag_lengths, first_core, middle_core, last_core, grad_hidden):
    nd, nt = lax.axis_size("dp"), lax.axis_size("table")
    block, hidden = grad_hidden.shape
    ncore = middle_core.shape[1]
    ids = jnp.transpose(core_ids, (1, 2, 3, 0))
    lengths = jnp.transpose(bag_lengths)
    cols = hidden // nd
    half = hidden // 2
    vmem = pl.BlockSpec(memory_space=pltpu.VMEM)
    hbm = pl.BlockSpec(memory_space=pltpu.HBM)
    dma = pltpu.SemaphoreType.DMA
    padded = ncore // 16 * 16 + 16
    return pl.pallas_call(
        functools.partial(kernel, nd, nt),
        out_shape=(
            jax.ShapeDtypeStruct((block, nt * WIDTH), BF16),
            jax.ShapeDtypeStruct((WIDTH, cols), F32),
        ),
        in_specs=[hbm] * 6,
        out_specs=(vmem, vmem),
        scratch_shapes=[
            pltpu.VMEM(ids.shape, jnp.int32),
            pltpu.VMEM(lengths.shape, jnp.int32),
            pltpu.VMEM((nt, 8, block), jnp.int32),
            pltpu.VMEM((nt, 8, block), jnp.int32),
            pltpu.SMEM((2, 8, block), jnp.int32),
            pltpu.VMEM((ncore, RANK, D2 * RANK), BF16),
            pltpu.VMEM((2, ncore, D1 * RANK), BF16),
            pltpu.VMEM((nt, block, half), BF16),
            pltpu.VMEM((nt, block, WIDTH), BF16),
            pltpu.VMEM((nt, block, WIDTH), BF16),
            pltpu.VMEM((padded, D1, LANES), F32),
            pltpu.VMEM((padded * D2 * D3, LANES), F32),
            pltpu.VMEM((padded, D2 * D3, LANES), BF16),
            pltpu.VMEM((block, LANES), F32),
            pltpu.VMEM((block, WIDTH), F32),
            pltpu.VMEM((2, nd // 2, WIDTH, cols), BF16),
            pltpu.VMEM((nd, WIDTH, cols), BF16),
            dma((2,)), dma, dma((2,)), dma, dma((2,)),
            dma((nt,)), dma((nt,)), dma((nt,)), dma((nt,)), dma((nt,)), dma((nt,)),
            dma((nt,)), dma((nt,)), dma((2, nd // 2)), dma((nd,)),
        ],
        compiler_params=pltpu.CompilerParams(
            collective_id=0, has_side_effects=True, vmem_limit_bytes=60 * 1024 * 1024
        ),
        cost_estimate=pl.CostEstimate(flops=2 * 10**9, bytes_accessed=6 * 10**6, transcendentals=0),
    )(ids, lengths, first_core[0], middle_core[0], last_core[0], grad_hidden)


def solution(mesh):
    placed = (
        P(("dp", "table"), None, None, None),
        P(("dp", "table"), None),
        P("table", None, None),
        P("table", None, None, None),
        P("table", None, None),
        P(("dp", "table"), None),
    )
    return jax.shard_map(
        body,
        mesh=mesh,
        in_specs=placed,
        out_specs=(P(("dp", "table"), None), P("table", "dp")),
        check_vma=False,
    )
```

time: 49.2 us -> 34.2 us (0.70)
  Pallas kernels: 40.2 us -> 30.1 us
  local copies, waits for them, and re-layouts: 7.19 us -> 3.24 us
  other arithmetic: 0.76 us -> 0 us
    pallas_call x1, Pallas kernels: 40.2 us -> 30.1 us  [body(): pl.pallas_call(functools.partial(kernel, nd, nt), out_shape=(jax.ShapeDty...]
    unnamed x11 -> x2, local copies, waits for them, and re-layouts: 7.11 us -> 3.24 us
    concatenate x1 -> x0, other arithmetic: 0.76 us -> none  [body(): jnp.concatenate([jnp.transpose(core_ids, (1, 2, 3, 0)).reshape(nt, 3 * BA...]
where the time goes in v2:
time: 34.2 us; the launch traced here: 34 us
  Pallas kernels  30.1 us (88%)
  local copies, waits for them, and re-layouts  3.24 us (9%)
  between operations  0.64 us (2%)
    pallas_call x1, Pallas kernels, body(): pl.pallas_call(functools.partial(kernel, nd, nt), out_shape=(jax.ShapeDty...  30.1 us
    unnamed x2, local copies, waits for them, and re-layouts  3.24 us

profile of v2, /device:TPU:1, one launch (start us, length us, event | category | flops | bytes accessed | tf_op | source)
XLA Modules:
  0.0 34.0 jit_solution(815136176820718192)
XLA Ops:
  0.6 30.1 %shard_map.77 = (bf16[128,1024]{1,0:T(8,128)(2,1)}, f32[128,256]{1,0:T(8,128)}) custom-call(s32[8,3,2,128]{3,2,1,0:T(2,128)} %bitcast.8, s32[8,128]{1,0:T(8,128)} %bitcast.9, bf16[250,512]{1,0:T(8,128)(2,1)} %bitcast.6, bf16[250,64,128]{2,1,0:T(8,128)(2,1)} %bitcast.5, bf16[250,512]{1,0:T(8,128)(2,1)} %bitcast.7, bf16[128,1024]{1,0:T(8,128)(2,1)} %grad.1), custom_call_target="tpu_custom_call" | custom-call | flops 2000000000 | bytes 6000000 | tf_op jit(solution)/shard_map/pallas_call | solution.py:309
  30.8 1.7 %copy.10 = bf16[128,1024]{1,0:T(8,128)(2,1)} copy(bf16[128,1024]{1,0:T(8,128)(2,1)} %get-tuple-element.4) | data formatting | bytes 524288
  32.4 1.6 %copy.11 = f32[128,256]{1,0:T(8,128)} copy(f32[128,256]{1,0:T(8,128)} %get-tuple-element.5) | data formatting | bytes 262144

commit v3 on v2

--- a/solution.py
+++ b/solution.py
@@ -27,19 +27,23 @@
 
 def spread_tables(first, last, firstx, wide, lastx):
     ncore, length = first.shape
-    row = iota((length, LANES), 0)
-    lane = lax.rem(iota((length, LANES), 1), RANK)
-    half = iota((ncore, LANES), 1) // RANK
     wide[0 : firstx.shape[0] * D1] = jnp.zeros((firstx.shape[0] * D1, LANES), F32)
-    for a in range(D1):
-        pick = (row == a * RANK + lane).astype(F32).astype(BF16)
-        wide[pl.ds(a, ncore, stride=D1), :] = jnp.dot(first[...], pick, preferred_element_type=F32)
+    lower = iota((ncore, LANES), 1) < RANK
+    for a in range(0, D1, 2):
+        both = first[:, a * RANK : (a + 2) * RANK].astype(F32)
+        turned = pltpu.roll(both, RANK, 1)
+        wide[pl.ds(a, ncore, stride=D1), :] = jnp.where(lower, both, turned)
+        wide[pl.ds(a + 1, ncore, stride=D1), :] = jnp.where(lower, turned, both)
     firstx[...] = wide[0 : firstx.shape[0] * D1].reshape(firstx.shape)
-    for c in range(D3):
-        pick = (row == lane * D3 + c).astype(F32).astype(BF16)
+    row, lane = iota((length, 2 * LANES), 0), iota((length, 2 * LANES), 1)
+    want = row - lax.rem(lane, RANK) * D3 - lane // LANES
+    for c in range(0, D3, 2):
+        pick = (want == c).astype(F32).astype(BF16)
         found = jnp.dot(last[...], pick, preferred_element_type=F32)
-        for b in range(D2):
-            wide[pl.ds(b * D3 + c, ncore, stride=D2 * D3), :] = jnp.where(half == b, found, 0.0)
+        for e in range(2):
+            one = found[:, e * LANES : (e + 1) * LANES]
+            wide[pl.ds(c + e, ncore, stride=D2 * D3), :] = jnp.where(lower, one, 0.0)
+            wide[pl.ds(D3 + c + e, ncore, stride=D2 * D3), :] = jnp.where(lower, 0.0, one)
     lastx[...] = wide[...].reshape(lastx.shape).astype(BF16)
 
 
@@ -85,20 +89,23 @@
     return total
 
 
-def lookups(smem, slot, firstx, middle, lastx, found, block):
+def lookups(smem, slot, firstx, middle, lastx, found, ordered, block):
     prefixes = {}
     count = block // 8
+    before = found[...].astype(BF16)
     for g in range(count + LAG):
+        if g == 2 * LAG:
+            done = unfold(before, ordered, block)
         if g < count:
             prefixes[g] = heads_of(smem, slot, firstx, middle, g * 8)
         if g >= LAG:
             h = g - LAG
             found[h * 8 : (h + 1) * 8, :] = tails_of(smem, slot, prefixes.pop(h), lastx, h * 8)
-
-
-def unfold(found, ordered, block):
+    return done
+
+
+def unfold(values, ordered, block):
     count = block // 8
-    values = found[...].astype(BF16)
     row, col = iota((LANES, SPAN), 0), iota((LANES, SPAN), 1)
     copies = jnp.logical_and(row // 16 == col // LANES, lax.rem(row, 16) == lax.rem(col, 16))
     copied = jnp.dot(values, copies.astype(F32).astype(BF16), preferred_element_type=F32)
@@ -205,22 +212,23 @@
                 device_id=(d, other), device_id_type=MESH).wait_recv()
             pltpu.make_async_copy(ids.at[after], smem.at[1 - slot], smem_sem.at[1 - slot]).start()
 
-        lookups(smem, slot, firstx, mid, lastx, found, block)
-        done = unfold(found, ordered, block)
-        rows[s] = done
-        send_sib(k).start()
+        rows[lax.rem(s + 1, nt)] = lookups(smem, slot, firstx, mid, lastx, found, ordered, block)
 
         @pl.when(k > 0)
         def _():
-            send_pooled(k).start()
-
-        @pl.when(k == 0)
+            send_sib(k - 1).start()
+
+        @pl.when(k > 1)
         def _():
-            pooled[:, pl.ds(pl.multiple_of(t * WIDTH, LANES), WIDTH)] = done
+            send_pooled(k - 1).start()
 
         return carry
 
     lax.fori_loop(0, nt, chunk, 0)
+    rows[lax.rem(t + 1, nt)] = unfold(found[...].astype(BF16), ordered, block)
+    send_sib(nt - 1).start()
+    send_pooled(nt - 1).start()
+    pooled[:, pl.ds(pl.multiple_of(t * WIDTH, LANES), WIDTH)] = rows[t]
     own.wait()
 
     for k in range(1, nt):
@@ -337,7 +345,7 @@
             dma((nt,)), dma((nt,)), dma((2, nd // 2)), dma((nd,)),
         ],
         compiler_params=pltpu.CompilerParams(
-            collective_id=0, has_side_effects=True, vmem_limit_bytes=60 * 1024 * 1024
+            collective_id=0, has_side_effects=True, vmem_limit_bytes=54784 * 1024
         ),
         cost_estimate=pl.CostEstimate(flops=2 * 10**9, bytes_accessed=6 * 10**6, transcendentals=0),
     )(ids, lengths, first_core[0], middle_core[0], last_core[0], grad_hidden)

time: 34.2 us -> 32.2 us (0.942)
  Pallas kernels: 30.1 us -> 28.6 us
  local copies, waits for them, and re-layouts: 3.24 us -> 2.78 us
    pallas_call x1, Pallas kernels: 30.1 us -> 28.6 us  [body(): pl.pallas_call(functools.partial(kernel, nd, nt), out_shape=(jax.ShapeDty...]
    unnamed x2 -> x6, local copies, waits for them, and re-layouts: 3.24 us -> 2.78 us
where the time goes in v3:
time: 32.2 us; the launch traced here: 32 us
  Pallas kernels  28.6 us (89%)
  local copies, waits for them, and re-layouts  2.78 us (9%)
  between operations  0.65 us (2%)
    pallas_call x1, Pallas kernels, body(): pl.pallas_call(functools.partial(kernel, nd, nt), out_shape=(jax.ShapeDty...  28.6 us
    unnamed x6, local copies, waits for them, and re-layouts  2.78 us

profile of v3, /device:TPU:1, one launch (start us, length us, event | category | flops | bytes accessed | tf_op | source)
XLA Modules:
  0.0 32.0 jit_solution(11979602372838937856)
XLA Ops:
  0.6 0.0 copy-start
  0.6 0.7 %copy-done = s32[128,8,3,2]{0,3,2,1:T(2,128)S(1)} copy-done((s32[128,8,3,2]{0,3,2,1:T(2,128)S(1)}, s32[128,8,3,2]{0,3,2,1:T(2,128)}, u32[]{:S(2)}) %copy-start) | copy-done | bytes 24600
  1.4 0.0 copy-start.1
  1.4 0.7 %copy-done.1 = s32[128,8]{0,1:T(8,128)S(1)} copy-done((s32[128,8]{0,1:T(8,128)S(1)}, s32[128,8]{0,1:T(8,128)}, u32[]{:S(2)}) %copy-start.1) | copy-done | bytes 4120
  2.1 28.6 %shard_map.77 = (bf16[128,1024]{1,0:T(8,128)(2,1)S(1)}, f32[128,256]{1,0:T(8,128)S(1)}) custom-call(s32[8,3,2,128]{3,2,1,0:T(2,128)S(1)} %bitcast.5, s32[8,128]{1,0:T(8,128)S(1)} %bitcast.6, bf16[250,512]{1,0:T(8,128)(2,1)} %bitcast.8, bf16[250,64,128]{2,1,0:T(8,128)(2,1)} %bitcast.7, bf16[250,512]{1,0:T(8,128)(2,1)} %bitcast.9, bf16[128,1024]{1,0:T(8,128)(2,1)} %grad.1), custom_call_target="tpu_custom_call" | custom-call | flops 2000000000 | bytes 6000000 | tf_op jit(solution)/shard_map/pallas_call | solution.py:317
  30.7 0.7 %copy.10 = bf16[128,1024]{1,0:T(8,128)(2,1)} copy(bf16[128,1024]{1,0:T(8,128)(2,1)S(1)} %get-tuple-element.4) | data formatting | bytes 524288
  31.4 0.7 %copy.11 = f32[128,256]{1,0:T(8,128)} copy(f32[128,256]{1,0:T(8,128)S(1)} %get-tuple-element.5) | data formatting | bytes 262144
Async XLA Ops:
  0.6 0.7 %copy-start = (s32[128,8,3,2]{0,3,2,1:T(2,128)S(1)}, s32[128,8,3,2]{0,3,2,1:T(2,128)}, u32[]{:S(2)}) copy-start(s32[128,8,3,2]{0,3,2,1:T(2,128)} %param.6) | copy-start | bytes 73732
  1.4 0.7 %copy-start.1 = (s32[128,8]{0,1:T(8,128)S(1)}, s32[128,8]{0,1:T(8,128)}, u32[]{:S(2)}) copy-start(s32[128,8]{0,1:T(8,128)} %param.7) | copy-start | bytes 12292

commit v4 on v3

--- a/solution.py
+++ b/solution.py
@@ -120,9 +120,9 @@
     return ordered[...].astype(BF16)
 
 
-def kernel(nd, nt, core_ids, lengths, first, middle, last, grad, pooled, wg,
-           raw_ids, raw_lengths, tiles, ids, smem, mid, ends, grads, rows, sib, firstx, wide, lastx, found, ordered, part, partin,
-           raw_sem, mid_sem, end_sem, own_sem, smem_sem, ids_ss, ids_rs, grad_ss, grad_rs, pool_ss, pool_rs, sib_ss, sib_rs,
+def kernel(nd, nt, raw_ids, first, middle, last, grad, pooled, wg,
+           tiles, ids, smem, mid, ends, grads, rows, sib, firstx, wide, lastx, found, ordered, part, partin,
+           mid_sem, end_sem, own_sem, smem_sem, ids_ss, ids_rs, grad_ss, grad_rs, pool_ss, pool_rs, sib_ss, sib_rs,
            part_ss, part_rs):
     d, t = lax.axis_index("dp"), lax.axis_index("table")
     core = lax.rem(t, 2)
@@ -136,9 +136,7 @@
 
     load = pltpu.make_async_copy(middle, mid, mid_sem)
     loads = [pltpu.make_async_copy(ref, ends.at[k], end_sem.at[k]) for k, ref in enumerate((first, last))]
-    raws = [pltpu.make_async_copy(core_ids, raw_ids, raw_sem.at[0]),
-            pltpu.make_async_copy(lengths, raw_lengths, raw_sem.at[1])]
-    for copy in raws + loads:
+    for copy in loads:
         copy.start()
     load.start()
 
@@ -153,50 +151,48 @@
     own = pltpu.make_async_copy(
         grad.at[:, pl.ds(pl.multiple_of(core * half, LANES), half)], grads.at[t], own_sem)
     own.start()
-    for copy in raws:
-        copy.wait()
     slots = iota((BAG, block), 0)
     for k in range(nt):
-        live = slots < raw_lengths[k : k + 1, :]
+        live = slots < raw_ids[k, 3]
         tiles[k, 0:BAG] = jnp.where(live, raw_ids[k, 0], ncore)
         tiles[k, BAG : 2 * BAG] = raw_ids[k, 1]
         tiles[k, 2 * BAG : 3 * BAG] = raw_ids[k, 2]
         tiles[k, 3 * BAG :] = jnp.zeros((8 - 3 * BAG, block), jnp.int32)
     pltpu.make_async_copy(tiles.at[t], smem.at[0], smem_sem.at[0]).start()
+    pl.semaphore_wait(barrier, nt - 1 + 2 * (nd - 1))
+
+    def send_ids(k):
+        peer = lax.rem(t + k, nt)
+        return pltpu.make_async_remote_copy(
+            tiles.at[peer], ids.at[t], ids_ss.at[k], ids_rs.at[k],
+            device_id=(d, peer), device_id_type=MESH)
+
+    def send_grad(k):
+        peer = lax.rem(t + k, nt)
+        mine = pl.ds(pl.multiple_of(lax.rem(peer, 2) * half, LANES), half)
+        return pltpu.make_async_remote_copy(
+            grad.at[:, mine], grads.at[t], grad_ss.at[k], grad_rs.at[k],
+            device_id=(d, peer), device_id_type=MESH)
+
+    def send_pooled(k):
+        peer = lax.rem(t - k + nt, nt)
+        return pltpu.make_async_remote_copy(
+            rows.at[peer], pooled.at[:, pl.ds(pl.multiple_of(t * WIDTH, LANES), WIDTH)],
+            pool_ss.at[k], pool_rs.at[k], device_id=(d, peer), device_id_type=MESH)
+
+    def send_sib(k):
+        peer = lax.rem(t - k + nt, nt)
+        return pltpu.make_async_remote_copy(
+            rows.at[peer], sib.at[peer], sib_ss.at[peer], sib_rs.at[peer],
+            device_id=(d, other), device_id_type=MESH)
+
+    for k in range(1, nt):
+        send_ids(k).start()
+    for k in range(1, nt):
+        send_grad(k).start()
     for copy in loads:
         copy.wait()
     spread_tables(ends.at[0], ends.at[1], firstx, wide, lastx)
-    pl.semaphore_wait(barrier, nt - 1 + 2 * (nd - 1))
-
-    def send_ids(k):
-        peer = lax.rem(t + k, nt)
-        return pltpu.make_async_remote_copy(
-            tiles.at[peer], ids.at[t], ids_ss.at[k], ids_rs.at[k],
-            device_id=(d, peer), device_id_type=MESH)
-
-    def send_grad(k):
-        peer = lax.rem(t + k, nt)
-        mine = pl.ds(pl.multiple_of(lax.rem(peer, 2) * half, LANES), half)
-        return pltpu.make_async_remote_copy(
-            grad.at[:, mine], grads.at[t], grad_ss.at[k], grad_rs.at[k],
-            device_id=(d, peer), device_id_type=MESH)
-
-    def send_pooled(k):
-        peer = lax.rem(t - k + nt, nt)
-        return pltpu.make_async_remote_copy(
-            rows.at[peer], pooled.at[:, pl.ds(pl.multiple_of(t * WIDTH, LANES), WIDTH)],
-            pool_ss.at[k], pool_rs.at[k], device_id=(d, peer), device_id_type=MESH)
-
-    def send_sib(k):
-        peer = lax.rem(t - k + nt, nt)
-        return pltpu.make_async_remote_copy(
-            rows.at[peer], sib.at[peer], sib_ss.at[peer], sib_rs.at[peer],
-            device_id=(d, other), device_id_type=MESH)
-
-    for k in range(1, nt):
-        send_ids(k).start()
-    for k in range(1, nt):
-        send_grad(k).start()
     load.wait()
 
     def chunk(k, carry):
@@ -236,11 +232,6 @@
         pltpu.make_async_remote_copy(
             grads.at[s], grads.at[s], grad_ss.at[k], grad_rs.at[k],
             device_id=(d, other), device_id_type=MESH).wait_recv()
-    for s in range(nt):
-        pltpu.make_async_remote_copy(
-            sib.at[s], sib.at[s], sib_ss.at[s], sib_rs.at[s],
-            device_id=(d, other), device_id_type=MESH).wait_recv()
-
     group = nt * block
 
     def partial(mine):
@@ -256,6 +247,11 @@
             device_id=(target, t if mine else other), device_id_type=MESH)
 
     for mine in (1, 0):
+        if not mine:
+            for s in range(nt):
+                pltpu.make_async_remote_copy(
+                    sib.at[s], sib.at[s], sib_ss.at[s], sib_rs.at[s],
+                    device_id=(d, other), device_id_type=MESH).wait_recv()
         whole = partial(mine)
         for q in range(per):
             part[mine, q] = whole[:, q * cols : (q + 1) * cols]
@@ -306,8 +302,8 @@
     nd, nt = lax.axis_size("dp"), lax.axis_size("table")
     block, hidden = grad_hidden.shape
     ncore = middle_core.shape[1]
-    ids = jnp.transpose(core_ids, (1, 2, 3, 0))
-    lengths = jnp.transpose(bag_lengths)
+    lengths = jnp.broadcast_to(jnp.transpose(bag_lengths)[:, None, None, :], (nt, 1, BAG, block))
+    ids = jnp.concatenate([jnp.transpose(core_ids, (1, 2, 3, 0)), lengths], axis=1)
     cols = hidden // nd
     half = hidden // 2
     vmem = pl.BlockSpec(memory_space=pltpu.VMEM)
@@ -320,11 +316,9 @@
             jax.ShapeDtypeStruct((block, nt * WIDTH), BF16),
             jax.ShapeDtypeStruct((WIDTH, cols), F32),
         ),
-        in_specs=[hbm] * 6,
+        in_specs=[vmem] + [hbm] * 4,
         out_specs=(vmem, vmem),
         scratch_shapes=[
-            pltpu.VMEM(ids.shape, jnp.int32),
-            pltpu.VMEM(lengths.shape, jnp.int32),
             pltpu.VMEM((nt, 8, block), jnp.int32),
             pltpu.VMEM((nt, 8, block), jnp.int32),
             pltpu.SMEM((2, 8, block), jnp.int32),
@@ -340,7 +334,7 @@
             pltpu.VMEM((block, WIDTH), F32),
             pltpu.VMEM((2, nd // 2, WIDTH, cols), BF16),
             pltpu.VMEM((nd, WIDTH, cols), BF16),
-            dma((2,)), dma, dma((2,)), dma, dma((2,)),
+            dma, dma((2,)), dma, dma((2,)),
             dma((nt,)), dma((nt,)), dma((nt,)), dma((nt,)), dma((nt,)), dma((nt,)),
             dma((nt,)), dma((nt,)), dma((2, nd // 2)), dma((nd,)),
         ],
@@ -348,7 +342,7 @@
             collective_id=0, has_side_effects=True, vmem_limit_bytes=54784 * 1024
         ),
         cost_estimate=pl.CostEstimate(flops=2 * 10**9, bytes_accessed=6 * 10**6, transcendentals=0),
-    )(ids, lengths, first_core[0], middle_core[0], last_core[0], grad_hidden)
+    )(ids, first_core[0], middle_core[0], last_core[0], grad_hidden)
 
 
 def solution(mesh):

time: 32.2 us -> 32 us (level)
  other arithmetic: 0 us -> 0.75 us
  local copies, waits for them, and re-layouts: 2.78 us -> 2.05 us
    unnamed x6 -> x2, local copies, waits for them, and re-layouts: 2.78 us -> 1.36 us
    concatenate x0 -> x1, other arithmetic: none -> 0.75 us  [body(): jnp.concatenate([jnp.transpose(core_ids, (1, 2, 3, 0)), lengths], axis=1)]
    broadcast_in_dim x0 -> x1, local copies, waits for them, and re-layouts: none -> 0.69 us  [body(): jnp.broadcast_to(jnp.transpose(bag_lengths)[:, None, None, :], (nt, 1, BA...]
where the time goes in v4:
time: 32 us; the launch traced here: 31.8 us
  Pallas kernels  28.3 us (88%)
  local copies, waits for them, and re-layouts  2.05 us (6%)
  other arithmetic  0.75 us (2%)
  between operations  0.64 us (2%)
    pallas_call x1, Pallas kernels, body(): pl.pallas_call(functools.partial(kernel, nd, nt), out_shape=(jax.ShapeDty...  28.3 us
    unnamed x2, local copies, waits for them, and re-layouts  1.36 us
    concatenate x1, other arithmetic, body(): jnp.concatenate([jnp.transpose(core_ids, (1, 2, 3, 0)), lengths], axis=1)  0.75 us
    broadcast_in_dim x1, local copies, waits for them, and re-layouts, body(): jnp.broadcast_to(jnp.transpose(bag_lengths)[:, None, None, :], (nt, 1, BA...  0.69 us

profile of v4, /device:TPU:1, one launch (start us, length us, event | category | flops | bytes accessed | tf_op | source)
XLA Modules:
  0.0 31.8 jit_solution(8920774258607156413)
XLA Ops:
  0.6 0.7 %broadcast_in_dim.2 = s32[8,1,2,128]{3,2,1,0:T(2,128)S(1)} broadcast(s32[8,128]{1,0:T(8,128)} %bitcast.6), dimensions={0,3} | broadcast | bytes 12288 | tf_op jit(solution)/shard_map/broadcast_in_dim | solution.py:305
  1.3 0.7 %pad_add_fusion.raw_ids = s32[8,4,2,128]{3,2,1,0:T(2,128)S(1)} fusion(s32[8,1,2,128]{3,2,1,0:T(2,128)S(1)} %broadcast_in_dim.2, s32[8,3,2,128]{3,2,1,0:T(2,128)} %bitcast.5), kind=kLoop, calls=%fused_computation | loop fusion | flops 8192 | bytes 65536 | tf_op jit(solution)/shard_map/concatenate | solution.py:306
  2.1 28.3 %shard_map.77 = (bf16[128,1024]{1,0:T(8,128)(2,1)S(1)}, f32[128,256]{1,0:T(8,128)S(1)}) custom-call(s32[8,4,2,128]{3,2,1,0:T(2,128)S(1)} %pad_add_fusion.raw_ids, bf16[250,512]{1,0:T(8,128)(2,1)} %bitcast.8, bf16[250,64,128]{2,1,0:T(8,128)(2,1)} %bitcast.7, bf16[250,512]{1,0:T(8,128)(2,1)} %bitcast.9, bf16[128,1024]{1,0:T(8,128)(2,1)} %grad.1), custom_call_target="tpu_custom_call" | custom-call | flops 2000000000 | bytes 6000000 | tf_op jit(solution)/shard_map/pallas_call | solution.py:313
  30.4 0.7 %copy.10 = bf16[128,1024]{1,0:T(8,128)(2,1)} copy(bf16[128,1024]{1,0:T(8,128)(2,1)S(1)} %get-tuple-element.4) | data formatting | bytes 524288
  31.1 0.7 %copy.11 = f32[128,256]{1,0:T(8,128)} copy(f32[128,256]{1,0:T(8,128)S(1)} %get-tuple-element.5) | data formatting | bytes 262144

commit v5 on v4

--- a/solution.py
+++ b/solution.py
@@ -89,18 +89,25 @@
     return total
 
 
-def lookups(smem, slot, firstx, middle, lastx, found, ordered, block):
-    prefixes = {}
+def finish(smem, slot, lastx, kept, found, block):
+    for e in range(LAG):
+        h = block // 8 - LAG + e
+        found[h * 8 : (h + 1) * 8, :] = tails_of(smem, slot, kept[e], lastx, h * 8)
+
+
+def lookups(smem, slot, old, firstx, middle, lastx, kept, found, ordered, block):
     count = block // 8
+    prefixes = {g: heads_of(smem, slot, firstx, middle, g * 8) for g in range(LAG)}
+    finish(smem, old, lastx, kept, found, block)
     before = found[...].astype(BF16)
-    for g in range(count + LAG):
+    for g in range(LAG, count):
+        prefixes[g] = heads_of(smem, slot, firstx, middle, g * 8)
+        h = g - LAG
+        found[h * 8 : (h + 1) * 8, :] = tails_of(smem, slot, prefixes.pop(h), lastx, h * 8)
         if g == 2 * LAG:
             done = unfold(before, ordered, block)
-        if g < count:
-            prefixes[g] = heads_of(smem, slot, firstx, middle, g * 8)
-        if g >= LAG:
-            h = g - LAG
-            found[h * 8 : (h + 1) * 8, :] = tails_of(smem, slot, prefixes.pop(h), lastx, h * 8)
+    for e in range(LAG):
+        kept[e] = prefixes.pop(count - LAG + e)
     return done
 
 
@@ -121,7 +128,7 @@
 
 
 def kernel(nd, nt, raw_ids, first, middle, last, grad, pooled, wg,
-           tiles, ids, smem, mid, ends, grads, rows, sib, firstx, wide, lastx, found, ordered, part, partin,
+           tiles, ids, smem, mid, ends, grads, rows, sib, firstx, wide, lastx, kept, found, ordered, part, partin,
            mid_sem, end_sem, own_sem, smem_sem, ids_ss, ids_rs, grad_ss, grad_rs, pool_ss, pool_rs, sib_ss, sib_rs,
            part_ss, part_rs):
     d, t = lax.axis_index("dp"), lax.axis_index("table")
@@ -129,7 +136,6 @@
     pair = t - core
     other = pair + 1 - core
     block = grad.shape[0]
-    ncore = middle.shape[0]
     half = grads.shape[2]
     cols = wg.shape[1]
     per = nd // 2
@@ -151,14 +157,16 @@
     own = pltpu.make_async_copy(
         grad.at[:, pl.ds(pl.multiple_of(core * half, LANES), half)], grads.at[t], own_sem)
     own.start()
-    slots = iota((BAG, block), 0)
     for k in range(nt):
-        live = slots < raw_ids[k, 3]
-        tiles[k, 0:BAG] = jnp.where(live, raw_ids[k, 0], ncore)
+        tiles[k, 0:BAG] = raw_ids[k, 0]
         tiles[k, BAG : 2 * BAG] = raw_ids[k, 1]
         tiles[k, 2 * BAG : 3 * BAG] = raw_ids[k, 2]
         tiles[k, 3 * BAG :] = jnp.zeros((8 - 3 * BAG, block), jnp.int32)
     pltpu.make_async_copy(tiles.at[t], smem.at[0], smem_sem.at[0]).start()
+    blank = pltpu.make_async_copy(tiles.at[t], smem.at[2], smem_sem.at[2])
+    blank.start()
+    kept[...] = jnp.zeros_like(kept)
+    found[...] = jnp.zeros_like(found)
     pl.semaphore_wait(barrier, nt - 1 + 2 * (nd - 1))
 
     def send_ids(k):
@@ -194,10 +202,11 @@
         copy.wait()
     spread_tables(ends.at[0], ends.at[1], firstx, wide, lastx)
     load.wait()
+    blank.wait()
 
     def chunk(k, carry):
         s = lax.rem(t - k + nt, nt)
-        slot = lax.rem(k, 2)
+        slot, after_slot, old = lax.rem(k, 3), lax.rem(k + 1, 3), lax.rem(k + 2, 3)
         pltpu.make_async_copy(ids.at[s], smem.at[slot], smem_sem.at[slot]).wait()
 
         @pl.when(k + 1 < nt)
@@ -206,9 +215,10 @@
             pltpu.make_async_remote_copy(
                 ids.at[after], ids.at[after], ids_ss.at[k + 1], ids_rs.at[k + 1],
                 device_id=(d, other), device_id_type=MESH).wait_recv()
-            pltpu.make_async_copy(ids.at[after], smem.at[1 - slot], smem_sem.at[1 - slot]).start()
-
-        rows[lax.rem(s + 1, nt)] = lookups(smem, slot, firstx, mid, lastx, found, ordered, block)
+            pltpu.make_async_copy(ids.at[after], smem.at[after_slot], smem_sem.at[after_slot]).start()
+
+        rows[lax.rem(s + 1, nt)] = lookups(
+            smem, slot, old, firstx, mid, lastx, kept, found, ordered, block)
 
         @pl.when(k > 0)
         def _():
@@ -221,6 +231,7 @@
         return carry
 
     lax.fori_loop(0, nt, chunk, 0)
+    finish(smem, lax.rem(nt - 1, 3), lastx, kept, found, block)
     rows[lax.rem(t + 1, nt)] = unfold(found[...].astype(BF16), ordered, block)
     send_sib(nt - 1).start()
     send_pooled(nt - 1).start()
@@ -302,8 +313,10 @@
     nd, nt = lax.axis_size("dp"), lax.axis_size("table")
     block, hidden = grad_hidden.shape
     ncore = middle_core.shape[1]
-    lengths = jnp.broadcast_to(jnp.transpose(bag_lengths)[:, None, None, :], (nt, 1, BAG, block))
-    ids = jnp.concatenate([jnp.transpose(core_ids, (1, 2, 3, 0)), lengths], axis=1)
+    ids = jnp.transpose(core_ids, (1, 2, 3, 0))
+    shape = (nt, 3, BAG, block)
+    unused = lax.broadcasted_iota(jnp.int32, shape, 2) >= jnp.transpose(bag_lengths)[:, None, None, :]
+    ids = jnp.where(jnp.logical_and(unused, lax.broadcasted_iota(jnp.int32, shape, 1) == 0), ncore, ids)
     cols = hidden // nd
     half = hidden // 2
     vmem = pl.BlockSpec(memory_space=pltpu.VMEM)
@@ -321,7 +334,7 @@
         scratch_shapes=[
             pltpu.VMEM((nt, 8, block), jnp.int32),
             pltpu.VMEM((nt, 8, block), jnp.int32),
-            pltpu.SMEM((2, 8, block), jnp.int32),
+            pltpu.SMEM((3, 8, block), jnp.int32),
             pltpu.VMEM((ncore, RANK, D2 * RANK), BF16),
             pltpu.VMEM((2, ncore, D1 * RANK), BF16),
             pltpu.VMEM((nt, block, half), BF16),
@@ -330,11 +343,12 @@
             pltpu.VMEM((padded, D1, LANES), F32),
             pltpu.VMEM((padded * D2 * D3, LANES), F32),
             pltpu.VMEM((padded, D2 * D3, LANES), BF16),
+            pltpu.VMEM((LAG, 8 * D1, BAG * LANES), BF16),
             pltpu.VMEM((block, LANES), F32),
             pltpu.VMEM((block, WIDTH), F32),
             pltpu.VMEM((2, nd // 2, WIDTH, cols), BF16),
             pltpu.VMEM((nd, WIDTH, cols), BF16),
-            dma, dma((2,)), dma, dma((2,)),
+            dma, dma((2,)), dma, dma((3,)),
             dma((nt,)), dma((nt,)), dma((nt,)), dma((nt,)), dma((nt,)), dma((nt,)),
             dma((nt,)), dma((nt,)), dma((2, nd // 2)), dma((nd,)),
         ],

time: 32 us -> 31.2 us (0.975)
  local copies, waits for them, and re-layouts: 2.05 us -> 1.36 us
    select_n x0 -> x1, other arithmetic: none -> 0.82 us  [body(): jnp.where(jnp.logical_and(unused, lax.broadcasted_iota(jnp.int32, shape,...]
    concatenate x1 -> x0, other arithmetic: 0.75 us -> none  [body(): jnp.concatenate([jnp.transpose(core_ids, (1, 2, 3, 0)), lengths], axis=1)]
    broadcast_in_dim x1 -> x0, local copies, waits for them, and re-layouts: 0.69 us -> none  [body(): jnp.broadcast_to(jnp.transpose(bag_lengths)[:, None, None, :], (nt, 1, BA...]
where the time goes in v5:
time: 31.2 us; the launch traced here: 31 us
  Pallas kernels  28.2 us (90%)
  local copies, waits for them, and re-layouts  1.36 us (4%)
  other arithmetic  0.83 us (3%)
  between operations  0.65 us (2%)
    pallas_call x1, Pallas kernels, body(): pl.pallas_call(functools.partial(kernel, nd, nt), out_shape=(jax.ShapeDty...  28.2 us
    unnamed x2, local copies, waits for them, and re-layouts  1.36 us
    select_n x1, other arithmetic, body(): jnp.where(jnp.logical_and(unused, lax.broadcasted_iota(jnp.int32, shape,...  0.82 us

profile of v5, /device:TPU:1, one launch (start us, length us, event | category | flops | bytes accessed | tf_op | source)
XLA Modules:
  0.0 31.0 jit_solution(2637055848553939452)
XLA Ops:
  0.6 0.8 %and_select_fusion.raw_ids = s32[8,3,2,128]{3,2,1,0:T(2,128)S(1)} fusion(s32[128,8,3,2]{0,3,2,1:T(2,128)} %param.6, pred[3]{0:T(512)(128)(4,1)S(1)} %iota_compare_fusion, s32[8,128]{1,0:T(8,128)} %bitcast.6), kind=kLoop, calls=%fused_computation | loop fusion | flops 18432 | bytes 53251 | tf_op jit(solution)/shard_map/jit(_where)/select_n | solution.py:319
  1.5 28.2 %shard_map.77 = (bf16[128,1024]{1,0:T(8,128)(2,1)S(1)}, f32[128,256]{1,0:T(8,128)S(1)}) custom-call(s32[8,3,2,128]{3,2,1,0:T(2,128)S(1)} %and_select_fusion.raw_ids, bf16[250,512]{1,0:T(8,128)(2,1)} %bitcast.8, bf16[250,64,128]{2,1,0:T(8,128)(2,1)} %bitcast.7, bf16[250,512]{1,0:T(8,128)(2,1)} %bitcast.9, bf16[128,1024]{1,0:T(8,128)(2,1)} %grad.1), custom_call_target="tpu_custom_call" | custom-call | flops 2000000000 | bytes 6000000 | tf_op jit(solution)/shard_map/pallas_call | solution.py:326
  29.6 0.7 %copy.10 = bf16[128,1024]{1,0:T(8,128)(2,1)} copy(bf16[128,1024]{1,0:T(8,128)(2,1)S(1)} %get-tuple-element.4) | data formatting | bytes 524288
  30.3 0.7 %copy.11 = f32[128,256]{1,0:T(8,128)} copy(f32[128,256]{1,0:T(8,128)S(1)} %get-tuple-element.5) | data formatting | bytes 262144
  (1 shorter events, 0.0 us)

commit v6 on v5

--- a/solution.py
+++ b/solution.py
@@ -231,25 +231,34 @@
         return carry
 
     lax.fori_loop(0, nt, chunk, 0)
+    own.wait()
+
+    for k in range(1, nt):
+        s = lax.rem(t - k + nt, nt)
+        pltpu.make_async_remote_copy(
+            grads.at[s], grads.at[s], grad_ss.at[k], grad_rs.at[k],
+            device_id=(d, other), device_id_type=MESH).wait_recv()
+    group = nt * block
+    final = lax.rem(t + 1, nt)
+
+    def early(left):
+        return lax.dot_general(
+            left[...].reshape(group, WIDTH), grads[...].reshape(group, half),
+            (((0,), (0,)), ((), ())), preferred_element_type=F32)
+
+    sums = early(rows)
     finish(smem, lax.rem(nt - 1, 3), lastx, kept, found, block)
     rows[lax.rem(t + 1, nt)] = unfold(found[...].astype(BF16), ordered, block)
     send_sib(nt - 1).start()
     send_pooled(nt - 1).start()
     pooled[:, pl.ds(pl.multiple_of(t * WIDTH, LANES), WIDTH)] = rows[t]
-    own.wait()
-
-    for k in range(1, nt):
-        s = lax.rem(t - k + nt, nt)
-        pltpu.make_async_remote_copy(
-            grads.at[s], grads.at[s], grad_ss.at[k], grad_rs.at[k],
-            device_id=(d, other), device_id_type=MESH).wait_recv()
-    group = nt * block
 
     def partial(mine):
-        left = rows if mine else sib
-        return lax.dot_general(
-            left[...].reshape(group, WIDTH), grads[...].reshape(group, half),
-            (((0,), (0,)), ((), ())), preferred_element_type=F32).astype(BF16)
+        if not mine:
+            return early(sib).astype(BF16)
+        more = lax.dot_general(
+            rows[final], grads[final], (((0,), (0,)), ((), ())), preferred_element_type=F32)
+        return (sums + more).astype(BF16)
 
     def send_part(mine, q):
         target = core * per + q

time: 31.2 us -> 31.3 us (level)
  no operation moved by 1% of the time
where the time goes in v6:
time: 31.3 us; the launch traced here: 31.1 us
  Pallas kernels  28.2 us (90%)
  local copies, waits for them, and re-layouts  1.36 us (4%)
  other arithmetic  0.83 us (3%)
  between operations  0.65 us (2%)
    pallas_call x1, Pallas kernels, body(): pl.pallas_call(functools.partial(kernel, nd, nt), out_shape=(jax.ShapeDty...  28.2 us
    unnamed x2, local copies, waits for them, and re-layouts  1.36 us
    select_n x1, other arithmetic, body(): jnp.where(jnp.logical_and(unused, lax.broadcasted_iota(jnp.int32, shape,...  0.82 us

profile of v6, /device:TPU:1, one launch (start us, length us, event | category | flops | bytes accessed | tf_op | source)
XLA Modules:
  0.0 31.1 jit_solution(7431601227883146173)
XLA Ops:
  0.6 0.8 %and_select_fusion.raw_ids = s32[8,3,2,128]{3,2,1,0:T(2,128)S(1)} fusion(s32[128,8,3,2]{0,3,2,1:T(2,128)} %param.6, pred[3]{0:T(512)(128)(4,1)S(1)} %iota_compare_fusion, s32[8,128]{1,0:T(8,128)} %bitcast.6), kind=kLoop, calls=%fused_computation | loop fusion | flops 18432 | bytes 53251 | tf_op jit(solution)/shard_map/jit(_where)/select_n | solution.py:328
  1.5 28.2 %shard_map.77 = (bf16[128,1024]{1,0:T(8,128)(2,1)S(1)}, f32[128,256]{1,0:T(8,128)S(1)}) custom-call(s32[8,3,2,128]{3,2,1,0:T(2,128)S(1)} %and_select_fusion.raw_ids, bf16[250,512]{1,0:T(8,128)(2,1)} %bitcast.8, bf16[250,64,128]{2,1,0:T(8,128)(2,1)} %bitcast.7, bf16[250,512]{1,0:T(8,128)(2,1)} %bitcast.9, bf16[128,1024]{1,0:T(8,128)(2,1)} %grad.1), custom_call_target="tpu_custom_call" | custom-call | flops 2000000000 | bytes 6000000 | tf_op jit(solution)/shard_map/pallas_call | solution.py:335
  29.7 0.7 %copy.10 = bf16[128,1024]{1,0:T(8,128)(2,1)} copy(bf16[128,1024]{1,0:T(8,128)(2,1)S(1)} %get-tuple-element.4) | data formatting | bytes 524288
  30.4 0.7 %copy.11 = f32[128,256]{1,0:T(8,128)} copy(f32[128,256]{1,0:T(8,128)S(1)} %get-tuple-element.5) | data formatting | bytes 262144
  (1 shorter events, 0.0 us)

commit v7 on v5

--- a/solution.py
+++ b/solution.py
@@ -53,7 +53,7 @@
     zero = jnp.zeros((16, LANES), BF16)
     groups = []
     for g in range(2):
-        lefts, rights = [], []
+        slots = []
         for j in range(BAG):
             heads, centres = [], []
             for i in range(4):
@@ -62,14 +62,10 @@
                 centres.append(middle[smem[slot, 2 + j, n]])
             top = jnp.concatenate(heads[:2], axis=0).astype(BF16)
             low = jnp.concatenate(heads[2:], axis=0).astype(BF16)
-            lefts.append(jnp.concatenate([top, zero], axis=1))
-            lefts.append(jnp.concatenate([zero, low], axis=1))
-            rights.append(jnp.concatenate(centres, axis=0))
-        both = jnp.dot(jnp.concatenate(lefts, axis=0), jnp.concatenate(rights, axis=1),
-                       preferred_element_type=F32)
-        groups.append(jnp.concatenate(
-            [both[j * 32 : (j + 1) * 32, j * LANES : (j + 1) * LANES] for j in range(BAG)], axis=1
-        ).astype(BF16))
+            left = jnp.concatenate(
+                [jnp.concatenate([top, zero], axis=1), jnp.concatenate([zero, low], axis=1)], axis=0)
+            slots.append(jnp.dot(left, jnp.concatenate(centres, axis=0), preferred_element_type=F32))
+        groups.append(jnp.concatenate(slots, axis=1).astype(BF16))
     return jnp.concatenate(groups, axis=0)
 
 

time: 31.2 us -> 31 us (level)
  no operation moved by 1% of the time
where the time goes in v7:
time: 31 us; the launch traced here: 30.8 us
  Pallas kernels  27.9 us (90%)
  local copies, waits for them, and re-layouts  1.36 us (4%)
  other arithmetic  0.83 us (3%)
  between operations  0.65 us (2%)
    pallas_call x1, Pallas kernels, body(): pl.pallas_call(functools.partial(kernel, nd, nt), out_shape=(jax.ShapeDty...  27.9 us
    unnamed x2, local copies, waits for them, and re-layouts  1.36 us
    select_n x1, other arithmetic, body(): jnp.where(jnp.logical_and(unused, lax.broadcasted_iota(jnp.int32, shape,...  0.82 us

profile of v7, /device:TPU:1, one launch (start us, length us, event | category | flops | bytes accessed | tf_op | source)
XLA Modules:
  0.0 30.8 jit_solution(5856999878042781369)
XLA Ops:
  0.6 0.8 %and_select_fusion.raw_ids = s32[8,3,2,128]{3,2,1,0:T(2,128)S(1)} fusion(s32[128,8,3,2]{0,3,2,1:T(2,128)} %param.6, pred[3]{0:T(512)(128)(4,1)S(1)} %iota_compare_fusion, s32[8,128]{1,0:T(8,128)} %bitcast.6), kind=kLoop, calls=%fused_computation | loop fusion | flops 18432 | bytes 53251 | tf_op jit(solution)/shard_map/jit(_where)/select_n | solution.py:315
  1.5 27.9 %shard_map.77 = (bf16[128,1024]{1,0:T(8,128)(2,1)S(1)}, f32[128,256]{1,0:T(8,128)S(1)}) custom-call(s32[8,3,2,128]{3,2,1,0:T(2,128)S(1)} %and_select_fusion.raw_ids, bf16[250,512]{1,0:T(8,128)(2,1)} %bitcast.8, bf16[250,64,128]{2,1,0:T(8,128)(2,1)} %bitcast.7, bf16[250,512]{1,0:T(8,128)(2,1)} %bitcast.9, bf16[128,1024]{1,0:T(8,128)(2,1)} %grad.1), custom_call_target="tpu_custom_call" | custom-call | flops 2000000000 | bytes 6000000 | tf_op jit(solution)/shard_map/pallas_call | solution.py:322
  29.4 0.7 %copy.10 = bf16[128,1024]{1,0:T(8,128)(2,1)} copy(bf16[128,1024]{1,0:T(8,128)(2,1)S(1)} %get-tuple-element.4) | data formatting | bytes 524288
  30.1 0.7 %copy.11 = f32[128,256]{1,0:T(8,128)} copy(f32[128,256]{1,0:T(8,128)S(1)} %get-tuple-element.5) | data formatting | bytes 262144
  (1 shorter events, 0.0 us)
